TPU v7x, 128 devices: a whole 4x4x4 slice. The times are simulated.
128 devices in a mesh: wide: 32 (over y, x_hi, z), narrow: 4 (over x_lo, core).
Axes of the slice: x: 4 (x_hi: 2, x_lo: 2; x = x_hi * 2 + x_lo), y: 4, z: 4, core: 2. Of those that a mesh axis runs over, the one named last changes fastest.
Arguments:
- tokens: bfloat16 [16384, 1536], P(('wide', 'narrow')), may hold values from -6 to 6
- lengths: int32 [128, 4], P(('wide', 'narrow')), may hold values from 0 to 128, as said below
- w_query: bfloat16 [1536, 1536], P('narrow'), may hold values from -0.15625 to 0.15625
- w_key: bfloat16 [1536, 1536], P('narrow'), may hold values from -0.15625 to 0.15625
- w_value: bfloat16 [1536, 1536], P('narrow'), may hold values from -0.15625 to 0.15625
- w_out: bfloat16 [1536, 1536], P('narrow'), may hold values from -0.625 to 0.625
- w_forget: bfloat16 [1536, 24], P('narrow'), may hold values from -0.15625 to 0.15625
- forget_bias: bfloat16 [24], P('narrow'), may hold values from 0.5 to 6
- norm_attn: bfloat16 [1536], P('narrow'), may hold values from 0.5 to 1.5
- w_gate: bfloat16 [1536, 4096], P('narrow'), may hold values from -0.15625 to 0.15625
- w_up: bfloat16 [1536, 4096], P('narrow'), may hold values from -0.15625 to 0.15625
- w_down: bfloat16 [4096, 1536], P('narrow'), may hold values from -0.09375 to 0.09375
- norm_ffn: bfloat16 [1536], P('narrow'), may hold values from 0.5 to 1.5
- cotangent: bfloat16 [16384, 1536], P(('wide', 'narrow')), may hold values from -6 to 6
Outputs:
- output: bfloat16 [16384, 1536], P(('wide', 'narrow'))
- grad_tokens: float32 [16384, 1536], P(('wide', 'narrow'))
- grad_query: float32 [1536, 1536], P('narrow')
- grad_key: float32 [1536, 1536], P('narrow')
- grad_value: float32 [1536, 1536], P('narrow')
- grad_out: float32 [1536, 1536], P('narrow')
- grad_forget: float32 [1536, 24], P('narrow')
- grad_bias: float32 [24], P('narrow')
- grad_norm_attn: float32 [1536], P('narrow')
- grad_gate: float32 [1536, 4096], P('narrow')
- grad_up: float32 [1536, 4096], P('narrow')
- grad_down: float32 [4096, 1536], P('narrow')
- grad_norm_ffn: float32 [1536], P('narrow')
Inputs may be any that keep to these rules, and one draw needn't show every extreme that they name: Each row's lengths sum to at most 128; slots of length 0 hold no sequence; in every draw some device holds a single sequence of 128 rows.
All inputs are finite; a program needn't handle non-finite values.
Results may differ from a plain program's by a relative error of at most 0.028.
Values may be sent and summed in bfloat16 or wider, within the bound.
No kernel may reach another device: no remote copies, remote signals or barrier semaphores. Data moves between devices by JAX's collectives and lax.ppermute only.
A program may use at most 448 MiB of HBM per device.

v0:
```python
import jax
import jax.numpy as jnp
from jax import lax
from jax.sharding import PartitionSpec as P

D = 1536
H = 24
HD = 64
SLOTS = 4


EPSILON = 1e-06


def matmul(former, latter):
    return jnp.dot(former, latter, preferred_element_type=jnp.float32)


def product_over_rows(former, latter):
    return lax.dot_general(
        former, latter, (((0,), (0,)), ((), ())), preferred_element_type=jnp.float32
    )


def product_by_transpose(former, latter):
    return lax.dot_general(
        former, latter, (((1,), (1,)), ((), ())), preferred_element_type=jnp.float32
    )


def norm_rows(values, gain_row):
    factor = lax.rsqrt(jnp.mean(values * values, axis=1, keepdims=True) + EPSILON)
    return (factor, values * factor * gain_row)


def norm_back(values, factor, gain_row, incoming):
    scaled = incoming * gain_row
    gain_grad = jnp.sum(incoming * values * factor, axis=0)
    inner_sum = jnp.mean(scaled * values, axis=1, keepdims=True)
    return (scaled * factor - values * (factor * factor * factor) * inner_sum, gain_grad)


def softmax_rows(queries, key_rows, decays, allowed, head_scale):
    scores = (
        jnp.einsum("ihd,jhd->hij", queries, key_rows, preferred_element_type=jnp.float32)
        * head_scale
    )
    scores = scores + decays.T[:, :, None] - decays.T[:, None, :]
    scores = jnp.where(allowed[None], scores, -1e30)
    highest = jnp.max(scores, axis=2, keepdims=True)
    weights = jnp.exp(scores - highest)
    return weights / jnp.sum(weights, axis=2, keepdims=True)


def body(
    tokens,
    lengths,
    w_query,
    w_key,
    w_value,
    w_out,
    w_forget,
    forget_bias,
    norm_attn,
    w_gate,
    w_up,
    w_down,
    norm_ffn,
    cotangent,
):
    row_count = tokens.shape[0]
    head_scale = HD ** (-0.5)
    seq_ends = jnp.cumsum(lengths[0])
    position = jnp.arange(row_count, dtype=jnp.int32)
    segment = jnp.sum((position[:, None] >= seq_ends[None, :]).astype(jnp.int32), axis=1)
    live_rows = (segment < SLOTS).astype(jnp.float32)[:, None]
    allowed = (position[:, None] >= position[None, :]) & (segment[:, None] == segment[None, :])
    inputs = tokens.astype(jnp.float32)
    full_query, full_key, full_value, full_out, full_forget, full_bias, full_norm_attn = (
        lax.all_gather(w_query, "narrow", axis=0, tiled=True),
        lax.all_gather(w_key, "narrow", axis=0, tiled=True),
        lax.all_gather(w_value, "narrow", axis=0, tiled=True),
        lax.all_gather(w_out, "narrow", axis=0, tiled=True),
        lax.all_gather(w_forget, "narrow", axis=0, tiled=True),
        lax.all_gather(forget_bias, "narrow", axis=0, tiled=True),
        lax.all_gather(norm_attn, "narrow", axis=0, tiled=True),
    )
    gain_one = full_norm_attn.astype(jnp.float32)
    factor_one, scaled_one = norm_rows(inputs, gain_one)
    normed = scaled_one.astype(jnp.bfloat16)
    queries = matmul(normed, full_query).astype(jnp.bfloat16).reshape(row_count, H, HD)
    key_rows = matmul(normed, full_key).astype(jnp.bfloat16).reshape(row_count, H, HD)
    values = matmul(normed, full_value).astype(jnp.bfloat16).reshape(row_count, H, HD)
    forget = matmul(normed, full_forget) + full_bias.astype(jnp.float32)
    decays = jnp.cumsum(jax.nn.log_sigmoid(forget), axis=0)
    attn_probs = softmax_rows(queries, key_rows, decays, allowed, head_scale)
    probs_low = attn_probs.astype(jnp.bfloat16)
    mixed_heads = jnp.einsum("hij,jhd->ihd", probs_low, values, preferred_element_type=jnp.float32)
    mixed = mixed_heads.astype(jnp.bfloat16).reshape(row_count, D)
    middle = inputs + matmul(mixed, full_out)
    full_gate, full_up, full_down, full_norm_ffn = (
        lax.all_gather(w_gate, "narrow", axis=0, tiled=True),
        lax.all_gather(w_up, "narrow", axis=0, tiled=True),
        lax.all_gather(w_down, "narrow", axis=0, tiled=True),
        lax.all_gather(norm_ffn, "narrow", axis=0, tiled=True),
    )
    gain_two = full_norm_ffn.astype(jnp.float32)
    factor_two, scaled_two = norm_rows(middle, gain_two)
    normed_two = scaled_two.astype(jnp.bfloat16)
    gate_pre = matmul(normed_two, full_gate)
    upward = matmul(normed_two, full_up)
    hidden = (jax.nn.silu(gate_pre) * upward).astype(jnp.bfloat16)
    output = (live_rows * (middle + matmul(hidden, full_down))).astype(jnp.bfloat16)
    back_gate, back_up, back_down = (
        lax.all_gather(w_gate, "narrow", axis=0, tiled=True),
        lax.all_gather(w_up, "narrow", axis=0, tiled=True),
        lax.all_gather(w_down, "narrow", axis=0, tiled=True),
    )
    grad_live = cotangent.astype(jnp.float32) * live_rows
    grad_branch = grad_live.astype(jnp.bfloat16)
    grad_hidden = product_by_transpose(grad_branch, back_down)
    gate_sigmoid = jax.nn.sigmoid(gate_pre)
    grad_gate_pre = (
        grad_hidden * upward * gate_sigmoid * (1.0 + gate_pre * (1.0 - gate_sigmoid))
    ).astype(jnp.bfloat16)
    grad_upward = (grad_hidden * gate_pre * gate_sigmoid).astype(jnp.bfloat16)
    incoming_two = product_by_transpose(grad_gate_pre, back_gate) + product_by_transpose(
        grad_upward, back_up
    )
    grad_middle_norm, grad_gain_two = norm_back(middle, factor_two, gain_two, incoming_two)
    grad_middle = grad_live + grad_middle_norm
    grad_down_full = product_over_rows(hidden, grad_branch)
    grad_gate_full = product_over_rows(normed_two, grad_gate_pre)
    grad_up_full = product_over_rows(normed_two, grad_upward)
    grad_gate, grad_up, grad_down, grad_norm_ffn = (
        lax.psum_scatter(grad_gate_full, "narrow", scatter_dimension=0, tiled=True),
        lax.psum_scatter(grad_up_full, "narrow", scatter_dimension=0, tiled=True),
        lax.psum_scatter(grad_down_full, "narrow", scatter_dimension=0, tiled=True),
        lax.psum_scatter(grad_gain_two, "narrow", scatter_dimension=0, tiled=True),
    )
    back_query, back_key, back_value, back_out, back_forget = (
        lax.all_gather(w_query, "narrow", axis=0, tiled=True),
        lax.all_gather(w_key, "narrow", axis=0, tiled=True),
        lax.all_gather(w_value, "narrow", axis=0, tiled=True),
        lax.all_gather(w_out, "narrow", axis=0, tiled=True),
        lax.all_gather(w_forget, "narrow", axis=0, tiled=True),
    )
    grad_attn_branch = grad_middle.astype(jnp.bfloat16)
    grad_mixed = (
        product_by_transpose(grad_attn_branch, back_out)
        .astype(jnp.bfloat16)
        .reshape(row_count, H, HD)
    )
    grad_probs = jnp.einsum("ihd,jhd->hij", grad_mixed, values, preferred_element_type=jnp.float32)
    inner_sum = jnp.sum(attn_probs * grad_probs, axis=2, keepdims=True)
    grad_scores = (attn_probs * (grad_probs - inner_sum)).astype(jnp.bfloat16)
    grad_queries = (
        (
            jnp.einsum("hij,jhd->ihd", grad_scores, key_rows, preferred_element_type=jnp.float32)
            * head_scale
        )
        .astype(jnp.bfloat16)
        .reshape(row_count, D)
    )
    grad_keys = (
        (
            jnp.einsum("hij,ihd->jhd", grad_scores, queries, preferred_element_type=jnp.float32)
            * head_scale
        )
        .astype(jnp.bfloat16)
        .reshape(row_count, D)
    )
    grad_values = (
        jnp.einsum("hij,ihd->jhd", probs_low, grad_mixed, preferred_element_type=jnp.float32)
        .astype(jnp.bfloat16)
        .reshape(row_count, D)
    )
    scores_wide = grad_scores.astype(jnp.float32)
    grad_decays = (jnp.sum(scores_wide, axis=2) - jnp.sum(scores_wide, axis=1)).T
    grad_logs = jnp.flip(jnp.cumsum(jnp.flip(grad_decays, 0), axis=0), 0)
    grad_forget_pre = (grad_logs * jax.nn.sigmoid(-forget)).astype(jnp.bfloat16)
    incoming_one = product_by_transpose(grad_queries, back_query) + product_by_transpose(
        grad_keys, back_key
    )
    incoming_one = (
        incoming_one
        + product_by_transpose(grad_values, back_value)
        + product_by_transpose(grad_forget_pre, back_forget)
    )
    grad_input_norm, grad_gain_one = norm_back(inputs, factor_one, gain_one, incoming_one)
    grad_tokens = grad_middle + grad_input_norm
    grad_out_full = product_over_rows(mixed, grad_attn_branch)
    grad_query_full = product_over_rows(normed, grad_queries)
    grad_key_full = product_over_rows(normed, grad_keys)
    grad_value_full = product_over_rows(normed, grad_values)
    grad_forget_full = product_over_rows(normed, grad_forget_pre)
    grad_bias_full = jnp.sum(grad_forget_pre.astype(jnp.float32), axis=0)
    grad_query, grad_key, grad_value, grad_out, grad_forget, grad_bias, grad_norm_attn = (
        lax.psum_scatter(grad_query_full, "narrow", scatter_dimension=0, tiled=True),
        lax.psum_scatter(grad_key_full, "narrow", scatter_dimension=0, tiled=True),
        lax.psum_scatter(grad_value_full, "narrow", scatter_dimension=0, tiled=True),
        lax.psum_scatter(grad_out_full, "narrow", scatter_dimension=0, tiled=True),
        lax.psum_scatter(grad_forget_full, "narrow", scatter_dimension=0, tiled=True),
        lax.psum_scatter(grad_bias_full, "narrow", scatter_dimension=0, tiled=True),
        lax.psum_scatter(grad_gain_one, "narrow", scatter_dimension=0, tiled=True),
    )
    (
        grad_query,
        grad_key,
        grad_value,
        grad_out,
        grad_forget,
        grad_bias,
        grad_norm_attn,
        grad_gate,
        grad_up,
        grad_down,
        grad_norm_ffn,
    ) = lax.psum(
        (
            grad_query,
            grad_key,
            grad_value,
            grad_out,
            grad_forget,
            grad_bias,
            grad_norm_attn,
            grad_gate,
            grad_up,
            grad_down,
            grad_norm_ffn,
        ),
        "wide",
    )
    return (
        output,
        grad_tokens,
        grad_query,
        grad_key,
        grad_value,
        grad_out,
        grad_forget,
        grad_bias,
        grad_norm_attn,
        grad_gate,
        grad_up,
        grad_down,
        grad_norm_ffn,
    )


def solution(mesh):
    placed = (
        P(("wide", "narrow"), None),
        P(("wide", "narrow"), None),
        P("narrow", None),
        P("narrow", None),
        P("narrow", None),
        P("narrow", None),
        P("narrow", None),
        P("narrow"),
        P("narrow"),
        P("narrow", None),
        P("narrow", None),
        P("narrow", None),
        P("narrow"),
        P(("wide", "narrow"), None),
    )
    return jax.shard_map(
        body,
        mesh=mesh,
        in_specs=placed,
        out_specs=(
            P(("wide", "narrow"), None),
            P(("wide", "narrow"), None),
            P("narrow", None),
            P("narrow", None),
            P("narrow", None),
            P("narrow", None),
            P("narrow", None),
            P("narrow"),
            P("narrow"),
            P("narrow", None),
            P("narrow", None),
            P("narrow", None),
            P("narrow"),
        ),
        check_vma=False,
    )
```

profile of v0, /device:TPU:1, one launch (start us, length us, event | category | flops | bytes accessed | tf_op | source)
XLA Modules:
  0.0 2324.3 jit_solution(5354458160869694440)
XLA Ops:
  13.5 6.4 all-reduce
  19.9 6.9 all-gather
  26.9 5.7 all_gather.45
  34.5 5.1 all-gather.1
  40.1 24.6 %all-gather.10.cloned.1.call-done = bf16[1536,1536]{1,0:T(8,128)(2,1)} async-done(((bf16[384,1536]{1,0:T(8,128)(2,1)}), bf16[1536,1536]{1,0:T(8,128)(2,1)}) %all-gather.10.cloned.1.call-update) | async-done | bytes 4718608 | tf_op jit(solution)/shard_map/all_gather | solution.py:82
  68.7 49.4 %all-gather.12.cloned.1.call-done = bf16[1536,1536]{1,0:T(8,128)(2,1)} async-done(((bf16[384,1536]{1,0:T(8,128)(2,1)}), bf16[1536,1536]{1,0:T(8,128)(2,1)}) %all-gather.12.cloned.1.call-update) | async-done | bytes 4718608 | tf_op jit(solution)/shard_map/all_gather | solution.py:80
  121.5 50.0 %all-gather.14.cloned.1.call-done = bf16[1536,1536]{1,0:T(8,128)(2,1)} async-done(((bf16[384,1536]{1,0:T(8,128)(2,1)}), bf16[1536,1536]{1,0:T(8,128)(2,1)}) %all-gather.14.cloned.1.call-update) | async-done | bytes 4718608 | tf_op jit(solution)/shard_map/all_gather | solution.py:81
  176.5 48.4 %all-gather.16.cloned.1.call-done = bf16[1536,1536]{1,0:T(8,128)(2,1)} async-done(((bf16[384,1536]{1,0:T(8,128)(2,1)}), bf16[1536,1536]{1,0:T(8,128)(2,1)}) %all-gather.16.cloned.1.call-update) | async-done | bytes 4718608 | tf_op jit(solution)/shard_map/all_gather | solution.py:83
  228.8 114.8 %all-gather.18.cloned.1.call-done = bf16[1536,4096]{1,0:T(8,128)(2,1)} async-done(((bf16[384,4096]{1,0:T(8,128)(2,1)}), bf16[1536,4096]{1,0:T(8,128)(2,1)}) %all-gather.18.cloned.1.call-update) | async-done | bytes 12582928 | tf_op jit(solution)/shard_map/all_gather | solution.py:102
  343.5 7.7 fusion.45
  351.2 111.0 %all-gather.20.cloned.1.call-done = bf16[1536,4096]{1,0:T(8,128)(2,1)} async-done(((bf16[384,4096]{1,0:T(8,128)(2,1)}), bf16[1536,4096]{1,0:T(8,128)(2,1)}) %all-gather.20.cloned.1.call-update) | async-done | bytes 12582928 | tf_op jit(solution)/shard_map/all_gather | solution.py:103
  462.2 7.7 fusion.46
  469.9 111.1 %all-gather.22.cloned.1.call-done = bf16[4096,1536]{1,0:T(8,128)(2,1)} async-done(((bf16[1024,1536]{1,0:T(8,128)(2,1)}), bf16[4096,1536]{1,0:T(8,128)(2,1)}) %all-gather.22.cloned.1.call-update) | async-done | bytes 12582928 | tf_op jit(solution)/shard_map/all_gather | solution.py:104
  581.0 11.8 multiply_convert_fusion
  592.8 10.4 fusion.47
  603.2 7.2 multiply_reduce_fusion.1
  622.6 5.2 fusion.37
  637.8 5.1 fusion.33
  648.9 11.5 fusion.49
  660.5 11.6 fusion.50
  673.4 11.5 fusion.22
  691.2 25.1 %reduce-scatter.9.cloned.1.call-done = f32[384,1536]{1,0:T(8,128)} async-done(((f32[1536,1536]{1,0:T(8,128)}), f32[384,1536]{1,0:T(8,128)}) %reduce-scatter.9.cloned.1.call-update) | async-done | bytes 2359312 | tf_op jit(solution)/shard_map/reduce_scatter | solution.py:199
  716.3 91.0 %reduce-scatter.11.cloned.1.call-done = f32[384,1536]{1,0:T(8,128)} async-done(((f32[1536,1536]{1,0:T(8,128)}), f32[384,1536]{1,0:T(8,128)}) %reduce-scatter.11.cloned.1.call-update) | async-done | bytes 2359312 | tf_op jit(solution)/shard_map/reduce_scatter | solution.py:200
  807.2 90.8 %reduce-scatter.13.cloned.1.call-done = f32[384,1536]{1,0:T(8,128)} async-done(((f32[1536,1536]{1,0:T(8,128)}), f32[384,1536]{1,0:T(8,128)}) %reduce-scatter.13.cloned.1.call-update) | async-done | bytes 2359312 | tf_op jit(solution)/shard_map/reduce_scatter | solution.py:201
  898.1 91.0 %reduce-scatter.15.cloned.1.call-done = f32[384,1536]{1,0:T(8,128)} async-done(((f32[1536,1536]{1,0:T(8,128)}), f32[384,1536]{1,0:T(8,128)}) %reduce-scatter.15.cloned.1.call-update) | async-done | bytes 2359312 | tf_op jit(solution)/shard_map/reduce_scatter | solution.py:202
  989.1 217.5 %reduce-scatter.19.cloned.1.call-done = f32[384,4096]{1,0:T(8,128)} async-done(((f32[1536,4096]{1,0:T(8,128)}), f32[384,4096]{1,0:T(8,128)}) %reduce-scatter.19.cloned.1.call-update) | async-done | bytes 6291472 | tf_op jit(solution)/shard_map/reduce_scatter | solution.py:136
  1206.5 217.8 %reduce-scatter.21.cloned.1.call-done = f32[384,4096]{1,0:T(8,128)} async-done(((f32[1536,4096]{1,0:T(8,128)}), f32[384,4096]{1,0:T(8,128)}) %reduce-scatter.21.cloned.1.call-update) | async-done | bytes 6291472 | tf_op jit(solution)/shard_map/reduce_scatter | solution.py:137
  1424.3 217.5 %reduce-scatter.23.cloned.1.call-done = f32[1024,1536]{1,0:T(8,128)} async-done(((f32[4096,1536]{1,0:T(8,128)}), f32[1024,1536]{1,0:T(8,128)}) %reduce-scatter.23.cloned.1.call-update) | async-done | bytes 6291472 | tf_op jit(solution)/shard_map/reduce_scatter | solution.py:138
  1656.6 10.7 all-reduce.6
  1669.9 7.1 fusion.2
  1677.0 168.7 %all-reduce.4 = (f32[384,24]{0,1:T(8,128)}, f32[6]{0:T(128)}, f32[384]{0:T(512)}, f32[384]{0:T(512)}) all-reduce(f32[384,24]{0,1:T(8,128)} %reduce-scatter.17.cloned.1.call-done, f32[6]{0:T(128)S(1)} %dynamic-slice.2, f32[384]{0:T(512)S(1)} %dynamic-slice.4, f32[384]{0:T(512)S(1)} %dynamic-slice.6), channel_id=1, replica_groups=mesh['wide'=32,'narrow'=4] {'wide'}, use_global_device_ids=true, to_apply=%region_22.23 | all-reduce | flops 9990 | bytes 79920 | tf_op jit(solution)/shard_map/psum | solution.py:219
  1845.7 451.3 %all-reduce.9.cloned.1.call-done = (f32[384,1536]{1,0:T(8,128)}, f32[384,1536]{1,0:T(8,128)}, f32[384,1536]{1,0:T(8,128)}, f32[384,1536]{1,0:T(8,128)}, f32[384,...) async-done(((f32[384,1536]{1,0:T(8,128)}, f32[384,1536]{1,0:T(8,128)}, f32[384,1536]{1,0:T(8,128)}, f32[384,1536]{1,0:T(8,128)}, f32[384,4096]{1,0:T(8,128)}, ...) | async-done | bytes 28311568 | tf_op jit(solution)/shard_map/psum | solution.py:219
  (184 shorter events, 96.0 us)
Async XLA Ops:
  7.2 57.5 %all-gather.10.cloned.1.call-start = ((), (), s32[]{:S(2)}) async-start(), calls=%async_computation.8 | async-start | bytes 5898240 | tf_op jit(solution)/shard_map/all_gather | solution.py:82
  7.9 110.2 %all-gather.12.cloned.1.call-start = ((), (), s32[]{:S(2)}) async-start(), calls=%async_computation.9 | async-start | bytes 5898240 | tf_op jit(solution)/shard_map/all_gather | solution.py:80
  8.7 162.9 %all-gather.14.cloned.1.call-start = ((), (), s32[]{:S(2)}) async-start(), calls=%async_computation.10 | async-start | bytes 5898240 | tf_op jit(solution)/shard_map/all_gather | solution.py:81
  9.4 215.5 %all-gather.16.cloned.1.call-start = ((), (), s32[]{:S(2)}) async-start(), calls=%async_computation.11 | async-start | bytes 5898240 | tf_op jit(solution)/shard_map/all_gather | solution.py:83
  10.0 333.5 %all-gather.18.cloned.1.call-start = ((), (), s32[]{:S(2)}) async-start(), calls=%async_computation.12 | async-start | bytes 15728640 | tf_op jit(solution)/shard_map/all_gather | solution.py:102
  10.6 9.4 copy-start.30
  10.6 16.3 copy-start.22
  10.6 22.0 copy-start.1
  10.6 451.6 %all-gather.20.cloned.1.call-start = ((), (), s32[]{:S(2)}) async-start(), calls=%async_computation.13 | async-start | bytes 15728640 | tf_op jit(solution)/shard_map/all_gather | solution.py:103
  11.2 23.3 %copy-start.31 = (bf16[384]{0:T(512)(128)(2,1)S(1)}, bf16[384]{0:T(512)(128)(2,1)}, u32[]{:S(2)}) copy-start(bf16[384]{0:T(512)(128)(2,1)} %param.26) | copy-start | bytes 2308
  11.2 28.5 %copy-start.34 = (s32[1,4]{1,0:T(1,128)S(1)}, s32[1,4]{1,0:T(1,128)}, u32[]{:S(2)}) copy-start(s32[1,4]{1,0:T(1,128)} %param.15) | copy-start | bytes 52
  11.2 569.8 %all-gather.22.cloned.1.call-start = ((), (), s32[]{:S(2)}) async-start(), calls=%async_computation.14 | async-start | bytes 15728640 | tf_op jit(solution)/shard_map/all_gather | solution.py:104
  12.0 704.3 %reduce-scatter.9.cloned.1.call-start = ((), (), s32[]{:S(2)}) async-start(), calls=%async_computation.15 | async-start | bytes 11796480 | tf_op jit(solution)/shard_map/reduce_scatter | solution.py:199
  40.0 541.0 %copy-start.25 = (f32[128]{0:T(128)}, f32[128]{0:T(128)S(1)}, u32[]{:S(2)}) copy-start(f32[128]{0:T(128)S(1)} %compare_convert_fusion) | copy-start | bytes 1540
  121.5 53.5 %copy-start.11 = (bf16[128,1536]{0,1:T(8,128)(2,1)}, bf16[128,1536]{0,1:T(8,128)(2,1)S(1)}, u32[]{:S(2)}) copy-start(bf16[128,1536]{0,1:T(8,128)(2,1)S(1)} %copy.69) | copy-start | bytes 1179652
  175.8 52.3 %copy-start.14 = (f32[24,128,128]{1,2,0:T(8,128)}, f32[24,128,128]{1,2,0:T(8,128)S(1)}, u32[]{:S(2)}) copy-start(f32[24,128,128]{1,2,0:T(8,128)S(1)} %get-tuple-element.48) | copy-start | bytes 4718596
  175.8 441.6 %copy-start.23 = (f32[24,128]{1,0:T(8,128)}, f32[24,128]{1,0:T(8,128)S(1)}, u32[]{:S(2)}) copy-start(f32[24,128]{1,0:T(8,128)S(1)} %get-tuple-element.47) | copy-start | bytes 36868
  176.5 51.6 %copy-start.9 = (bf16[24,64,128]{2,1,0:T(8,128)(2,1)}, bf16[24,64,128]{2,1,0:T(8,128)(2,1)S(1)}, u32[]{:S(2)}) copy-start(bf16[24,64,128]{2,1,0:T(8,128)(2,1)S(1)} %convolution_convert_fusion.5) | copy-start | bytes 1179652
  228.6 114.9 %copy-start.28 = (f32[128]{0:T(128)}, f32[128]{0:T(128)S(1)}, u32[]{:S(2)}) copy-start(f32[128]{0:T(128)S(1)} %get-tuple-element.44) | copy-start | bytes 1540
  351.2 229.8 %copy-start.16 = (bf16[128,1536]{1,0:T(8,128)(2,1)S(1)}, bf16[128,1536]{1,0:T(8,128)(2,1)}, u32[]{:S(2)}) copy-start(bf16[128,1536]{1,0:T(8,128)(2,1)} %param.27) | copy-start | bytes 1179652
  592.8 10.4 copy-start
  627.9 179.4 %reduce-scatter.11.cloned.1.call-start = ((), (), s32[]{:S(2)}) async-start(), calls=%async_computation.16 | async-start | bytes 11796480 | tf_op jit(solution)/shard_map/reduce_scatter | solution.py:200
  634.9 263.2 %reduce-scatter.13.cloned.1.call-start = ((), (), s32[]{:S(2)}) async-start(), calls=%async_computation.17 | async-start | bytes 11796480 | tf_op jit(solution)/shard_map/reduce_scatter | solution.py:201
  642.9 346.2 %reduce-scatter.15.cloned.1.call-start = ((), (), s32[]{:S(2)}) async-start(), calls=%async_computation.18 | async-start | bytes 11796480 | tf_op jit(solution)/shard_map/reduce_scatter | solution.py:202
  648.9 557.7 %reduce-scatter.19.cloned.1.call-start = ((), (), s32[]{:S(2)}) async-start(), calls=%async_computation.20 | async-start | bytes 31457280 | tf_op jit(solution)/shard_map/reduce_scatter | solution.py:136
  660.5 763.8 %reduce-scatter.21.cloned.1.call-start = ((), (), s32[]{:S(2)}) async-start(), calls=%async_computation.21 | async-start | bytes 31457280 | tf_op jit(solution)/shard_map/reduce_scatter | solution.py:137
  672.2 969.6 %reduce-scatter.23.cloned.1.call-start = ((), (), s32[]{:S(2)}) async-start(), calls=%async_computation.22 | async-start | bytes 31457280 | tf_op jit(solution)/shard_map/reduce_scatter | solution.py:138
  685.0 992.0 %reduce-scatter.17.cloned.1.call-start = ((), (), s32[]{:S(2)}) async-start(), calls=%async_computation.19 | async-start | bytes 184320 | tf_op jit(solution)/shard_map/reduce_scatter | solution.py:203
  690.9 1606.1 %all-reduce.9.cloned.1.call-start = ((), (), s32[]{:S(2)}) async-start(), calls=%async_computation.23 | async-start | bytes 56623104 | tf_op jit(solution)/shard_map/psum | solution.py:219
  1651.3 16.2 copy-start.32
  1655.3 14.6 copy-start.27
  2306.3 7.5 slice-start
  (25 other events, 75.1 us)
Sparse Core Ops, SparseCore 0:
  9.7 54.9 all-gather.9
  66.3 51.7 all-gather.11
  119.8 51.7 all-gather.13
  173.1 51.7 all-gather.15
  226.4 117.1 all-gather.17
  345.0 117.1 all-gather.19
  463.9 117.1 all-gather.21
  628.0 88.2 reduce-scatter.8
  718.8 88.4 reduce-scatter.10
  809.6 88.4 reduce-scatter.12
  900.5 88.4 reduce-scatter.14
  991.4 215.0 reduce-scatter.18
  1209.2 215.0 reduce-scatter.20
  1426.6 215.0 reduce-scatter.22
  1644.7 18.0 reduce-scatter.16
  1665.7 631.2 all-reduce.8
where the time goes:
time: 2340 us; the launch traced here: 2320 us
  waiting for transfers between devices  1920 us (82%)
  blocking collectives  204 us (9%)
  matrix products  146 us (6%)
  local copies, waits for them, and re-layouts  30 us (1%)
    psum x1, waiting for transfers between devices, body(): lax.psum((grad_query, grad_key, grad_value, grad_out, grad_forget, grad_b...  451 us
    reduce_scatter x1, waiting for transfers between devices, body(): lax.psum_scatter(grad_up_full, 'narrow', scatter_dimension=0, tiled=True)  218 us
    reduce_scatter x1, waiting for transfers between devices, body(): lax.psum_scatter(grad_gate_full, 'narrow', scatter_dimension=0, tiled=True)  217 us
    reduce_scatter x1, waiting for transfers between devices, body(): lax.psum_scatter(grad_down_full, 'narrow', scatter_dimension=0, tiled=True)  217 us
    psum x1, blocking collectives, body(): lax.psum((grad_query, grad_key, grad_value, grad_out, grad_forget, grad_b...  169 us
    all_gather x1, waiting for transfers between devices, body(): lax.all_gather(w_gate, 'narrow', axis=0, tiled=True)  115 us
    all_gather x1, waiting for transfers between devices, body(): lax.all_gather(w_down, 'narrow', axis=0, tiled=True)  111 us
    all_gather x1, waiting for transfers between devices, body(): lax.all_gather(w_up, 'narrow', axis=0, tiled=True)  111 us
  transfers between devices with their start and end apart: 16, of which 15 were waited for; matrix products, arithmetic and copies ran while one was open for 5% of the time, Pallas kernels for 0%

commit v1 on v0

v1 whole, which is shorter than its diff:
```python
import functools

import jax
import jax.numpy as jnp
from jax import lax
from jax.experimental import pallas as pl
from jax.experimental.pallas import tpu as pltpu
from jax.sharding import Mesh, PartitionSpec as P

D = 1536
H = 24
HD = 64
FF = 4096
ROWS = 128
SLOTS = 4
EPSILON = 1e-06
SHARD = D // 4
FSHARD = FF // 4
LOCAL_HEADS = H // 4
WIDTH = 3 * SHARD + 128
AXES = ("y", "xh", "z", "xl", "c")
PLANE = ("y", "z")
F32 = jnp.float32
BF16 = jnp.bfloat16


def dot(former, latter, dims):
    return lax.dot_general(former, latter, (dims, ((), ())), preferred_element_type=F32)


AB = ((1,), (0,))
ABT = ((1,), (1,))
ATB = ((0,), (0,))


def exact_dot(former, latter):
    return lax.dot_general(
        former, latter, ((AB), ((), ())), precision=lax.Precision.HIGHEST, preferred_element_type=F32
    )


def attend_mask(lens_ref, block):
    rows = lax.broadcasted_iota(jnp.int32, (ROWS, ROWS), 0)
    cols = lax.broadcasted_iota(jnp.int32, (ROWS, ROWS), 1)
    seg_rows = jnp.zeros((ROWS, ROWS), jnp.int32)
    seg_cols = jnp.zeros((ROWS, ROWS), jnp.int32)
    end = jnp.int32(0)
    for slot in range(SLOTS):
        end = end + lens_ref[block, slot]
        seg_rows = seg_rows + (rows >= end).astype(jnp.int32)
        seg_cols = seg_cols + (cols >= end).astype(jnp.int32)
    return (rows >= cols) & (seg_rows == seg_cols)


def half_masks():
    lane = lax.broadcasted_iota(jnp.int32, (ROWS, 128), 1)
    return lane < HD, lane >= HD


def forward_kernel(
    lens_ref, x_ref, gain_ref, w_ref, bias_ref, wo_ref,
    keep_ref, send_ref, normed_ref, qkv_ref, forget_ref, probs_ref, mixed_ref,
):
    block = pl.program_id(0)
    x = x_ref[...].astype(F32)
    factor = lax.rsqrt(jnp.mean(x * x, axis=1, keepdims=True) + EPSILON)
    normed = (x * factor * gain_ref[...]).astype(BF16)
    normed_ref[...] = normed
    proj = dot(normed, w_ref[...], AB)
    qkv = proj[:, : 3 * SHARD].astype(BF16)
    qkv_ref[...] = qkv
    forget = proj[:, 3 * SHARD :] + bias_ref[...]
    forget_ref[...] = forget
    logs = jax.nn.log_sigmoid(forget)
    rows = lax.broadcasted_iota(jnp.int32, (ROWS, ROWS), 0)
    cols = lax.broadcasted_iota(jnp.int32, (ROWS, ROWS), 1)
    decays = exact_dot((rows >= cols).astype(F32), logs)
    decays_t = decays.T
    allowed = attend_mask(lens_ref, block)
    halves = half_masks()
    parts = []
    for pair in range(LOCAL_HEADS // 2):
        q2 = qkv[:, 128 * pair : 128 * pair + 128]
        k2 = qkv[:, SHARD + 128 * pair : SHARD + 128 * pair + 128]
        v2 = qkv[:, 2 * SHARD + 128 * pair : 2 * SHARD + 128 * pair + 128]
        total = jnp.zeros((ROWS, 128), F32)
        for side in range(2):
            head = 2 * pair + side
            kh = jnp.where(halves[side], k2, jnp.zeros_like(k2))
            vh = jnp.where(halves[side], v2, jnp.zeros_like(v2))
            scores = dot(q2, kh, ABT) * (HD ** (-0.5))
            scores = scores + decays[:, head : head + 1] - decays_t[head : head + 1, :]
            scores = jnp.where(allowed, scores, -1e30)
            highest = jnp.max(scores, axis=1, keepdims=True)
            weights = jnp.exp(scores - highest)
            probs = weights / jnp.sum(weights, axis=1, keepdims=True)
            probs_ref[0, head] = probs
            total = total + dot(probs.astype(BF16), vh, AB)
        parts.append(total.astype(BF16))
    mixed = jnp.concatenate(parts, axis=1)
    mixed_ref[...] = mixed
    partial = dot(mixed, wo_ref[...], AB).astype(BF16)

    @pl.when(block < 2)
    def _():
        keep_ref[...] = partial

    @pl.when(block >= 2)
    def _():
        send_ref[...] = partial


def attention_forward(lens, x, gain, w, bias, wo):
    whole = lambda b: (0, 0)
    row = lambda b: (b, 0)
    return pl.pallas_call(
        forward_kernel,
        grid=(4,),
        in_specs=[
            pl.BlockSpec(memory_space=pltpu.SMEM),
            pl.BlockSpec((ROWS, D), row),
            pl.BlockSpec((1, D), whole),
            pl.BlockSpec((D, WIDTH), whole),
            pl.BlockSpec((1, 128), whole),
            pl.BlockSpec((SHARD, D), whole),
        ],
        out_specs=[
            pl.BlockSpec((ROWS, D), lambda b: (jnp.minimum(b, 1), 0)),
            pl.BlockSpec((ROWS, D), lambda b: (jnp.maximum(b - 2, 0), 0)),
            pl.BlockSpec((ROWS, D), row),
            pl.BlockSpec((ROWS, 3 * SHARD), row),
            pl.BlockSpec((ROWS, 128), row),
            pl.BlockSpec((1, LOCAL_HEADS, ROWS, ROWS), lambda b: (b, 0, 0, 0)),
            pl.BlockSpec((ROWS, SHARD), row),
        ],
        out_shape=[
            jax.ShapeDtypeStruct((2 * ROWS, D), BF16),
            jax.ShapeDtypeStruct((2 * ROWS, D), BF16),
            jax.ShapeDtypeStruct((4 * ROWS, D), BF16),
            jax.ShapeDtypeStruct((4 * ROWS, 3 * SHARD), BF16),
            jax.ShapeDtypeStruct((4 * ROWS, 128), F32),
            jax.ShapeDtypeStruct((4, LOCAL_HEADS, ROWS, ROWS), F32),
            jax.ShapeDtypeStruct((4 * ROWS, SHARD), BF16),
        ],
        compiler_params=pltpu.CompilerParams(vmem_limit_bytes=40 * 1024 * 1024),
        cost_estimate=pl.CostEstimate(
            flops=2 * 4 * ROWS * D * (WIDTH + SHARD), bytes_accessed=16 * 1024 * 1024, transcendentals=400000
        ),
    )(lens, x, gain, w, bias, wo)


def backward_kernel(
    x_ref, gain_ref, gab_ref, wo_ref, qkv_ref, forget_ref, probs_ref, w_ref,
    keep_ref, send_ref, dqkvf_ref, gain_grad_ref,
):
    block = pl.program_id(0)
    gm = dot(gab_ref[...], wo_ref[...], ABT).astype(BF16)
    qkv = qkv_ref[...]
    halves = half_masks()
    lane = lax.broadcasted_iota(jnp.int32, (ROWS, 128), 1)
    rows = lax.broadcasted_iota(jnp.int32, (ROWS, ROWS), 0)
    cols = lax.broadcasted_iota(jnp.int32, (ROWS, ROWS), 1)
    grad_decays = jnp.zeros((ROWS, 128), F32)
    dqs, dks, dvs = [], [], []
    for pair in range(LOCAL_HEADS // 2):
        q2 = qkv[:, 128 * pair : 128 * pair + 128]
        k2 = qkv[:, SHARD + 128 * pair : SHARD + 128 * pair + 128]
        v2 = qkv[:, 2 * SHARD + 128 * pair : 2 * SHARD + 128 * pair + 128]
        g2 = gm[:, 128 * pair : 128 * pair + 128]
        dq = jnp.zeros((ROWS, 128), F32)
        dk = jnp.zeros((ROWS, 128), F32)
        dv = jnp.zeros((ROWS, 128), F32)
        for side in range(2):
            head = 2 * pair + side
            zero = jnp.zeros_like(q2)
            gh = jnp.where(halves[side], g2, zero)
            probs = probs_ref[0, head]
            grad_probs = dot(gh, v2, ABT)
            inner = jnp.sum(probs * grad_probs, axis=1, keepdims=True)
            ds = (probs * (grad_probs - inner)).astype(BF16)
            dq = dq + dot(ds, jnp.where(halves[side], k2, zero), AB)
            dk = dk + dot(ds, jnp.where(halves[side], q2, zero), ATB)
            dv = dv + dot(probs.astype(BF16), gh, ATB)
            pick = (lane == head).astype(BF16)
            grad_decays = grad_decays + dot(ds, pick, AB) - dot(ds, pick, ATB)
        dqs.append((dq * (HD ** (-0.5))).astype(BF16))
        dks.append((dk * (HD ** (-0.5))).astype(BF16))
        dvs.append(dv.astype(BF16))
    grad_logs = exact_dot((rows <= cols).astype(F32), grad_decays)
    grad_forget = (grad_logs * jax.nn.sigmoid(-forget_ref[...])).astype(BF16)
    dqkvf = jnp.concatenate(dqs + dks + dvs + [grad_forget], axis=1)
    dqkvf_ref[...] = dqkvf
    incoming = dot(dqkvf, w_ref[...], ABT)
    x = x_ref[...].astype(F32)
    factor = lax.rsqrt(jnp.mean(x * x, axis=1, keepdims=True) + EPSILON)
    gain_part = jnp.sum(incoming * x * factor, axis=0, keepdims=True)

    @pl.when(block == 0)
    def _():
        gain_grad_ref[...] = gain_part

    @pl.when(block > 0)
    def _():
        gain_grad_ref[...] = gain_grad_ref[...] + gain_part

    low = incoming.astype(BF16)

    @pl.when(block < 2)
    def _():
        keep_ref[...] = low

    @pl.when(block >= 2)
    def _():
        send_ref[...] = low


def attention_backward(x, gain, gab, wo, qkv, forget, probs, w):
    whole = lambda b: (0, 0)
    row = lambda b: (b, 0)
    return pl.pallas_call(
        backward_kernel,
        grid=(4,),
        in_specs=[
            pl.BlockSpec((ROWS, D), row),
            pl.BlockSpec((1, D), whole),
            pl.BlockSpec((ROWS, D), row),
            pl.BlockSpec((SHARD, D), whole),
            pl.BlockSpec((ROWS, 3 * SHARD), row),
            pl.BlockSpec((ROWS, 128), row),
            pl.BlockSpec((1, LOCAL_HEADS, ROWS, ROWS), lambda b: (b, 0, 0, 0)),
            pl.BlockSpec((D, WIDTH), whole),
        ],
        out_specs=[
            pl.BlockSpec((ROWS, D), lambda b: (jnp.minimum(b, 1), 0)),
            pl.BlockSpec((ROWS, D), lambda b: (jnp.maximum(b - 2, 0), 0)),
            pl.BlockSpec((ROWS, WIDTH), row),
            pl.BlockSpec((1, D), whole),
        ],
        out_shape=[
            jax.ShapeDtypeStruct((2 * ROWS, D), BF16),
            jax.ShapeDtypeStruct((2 * ROWS, D), BF16),
            jax.ShapeDtypeStruct((4 * ROWS, WIDTH), BF16),
            jax.ShapeDtypeStruct((1, D), F32),
        ],
        compiler_params=pltpu.CompilerParams(vmem_limit_bytes=40 * 1024 * 1024),
        cost_estimate=pl.CostEstimate(
            flops=2 * 4 * ROWS * D * (WIDTH + SHARD), bytes_accessed=16 * 1024 * 1024, transcendentals=70000
        ),
    )(x, gain, gab, wo, qkv, forget, probs, w)


FBLOCK = 256


def ffn_kernel(
    n2_ref, gb_ref, wg_ref, wu_ref, wd_ref,
    keep_ref, send_ref, hidden_ref, dg_ref, du_ref, total_ref,
):
    step = pl.program_id(0)
    n2 = n2_ref[...]
    wg, wu = wg_ref[...], wu_ref[...]
    gate = dot(n2, wg, AB)
    up = dot(n2, wu, AB)
    grad_hidden = dot(gb_ref[...], wd_ref[...], ABT)
    sig = jax.nn.sigmoid(gate)
    act = gate * sig
    hidden_ref[...] = (act * up).astype(BF16)
    dg = (grad_hidden * up * sig * (1.0 + gate * (1.0 - sig))).astype(BF16)
    du = (grad_hidden * act).astype(BF16)
    dg_ref[...] = dg
    du_ref[...] = du
    part = dot(dg, wg, ABT) + dot(du, wu, ABT)

    @pl.when(step == 0)
    def _():
        total_ref[...] = part

    @pl.when(step > 0)
    def _():
        total_ref[...] = total_ref[...] + part

    @pl.when(step == pl.num_programs(0) - 1)
    def _():
        keep_ref[...] = total_ref[: 2 * ROWS, :].astype(BF16)
        send_ref[...] = total_ref[2 * ROWS :, :].astype(BF16)


def ffn(n2, gb, wgu, wd):
    whole = lambda b: (0, 0)
    col = lambda b: (0, b)
    steps = FSHARD // FBLOCK
    return pl.pallas_call(
        ffn_kernel,
        grid=(steps,),
        in_specs=[
            pl.BlockSpec((4 * ROWS, D), whole),
            pl.BlockSpec((4 * ROWS, D), whole),
            pl.BlockSpec((D, FBLOCK), col),
            pl.BlockSpec((D, FBLOCK), lambda b: (0, steps + b)),
            pl.BlockSpec((FBLOCK, D), lambda b: (b, 0)),
        ],
        out_specs=[
            pl.BlockSpec((2 * ROWS, D), whole),
            pl.BlockSpec((2 * ROWS, D), whole),
            pl.BlockSpec((4 * ROWS, FBLOCK), col),
            pl.BlockSpec((4 * ROWS, FBLOCK), col),
            pl.BlockSpec((4 * ROWS, FBLOCK), col),
        ],
        out_shape=[
            jax.ShapeDtypeStruct((2 * ROWS, D), BF16),
            jax.ShapeDtypeStruct((2 * ROWS, D), BF16),
            jax.ShapeDtypeStruct((4 * ROWS, FSHARD), BF16),
            jax.ShapeDtypeStruct((4 * ROWS, FSHARD), BF16),
            jax.ShapeDtypeStruct((4 * ROWS, FSHARD), BF16),
        ],
        scratch_shapes=[pltpu.VMEM((4 * ROWS, D), F32)],
        compiler_params=pltpu.CompilerParams(vmem_limit_bytes=48 * 1024 * 1024),
        cost_estimate=pl.CostEstimate(
            flops=2 * 4 * ROWS * D * FSHARD * 5, bytes_accessed=18 * 1024 * 1024, transcendentals=4 * ROWS * FSHARD
        ),
    )(n2, gb, wgu, wgu, wd)


def make_body(sizes):
    ny, nxh, nz = sizes
    np_ = ny * nz

    def send(value, move):
        pairs = []
        for y in range(ny):
            for x in range(2 * nxh):
                for z in range(nz):
                    for c in range(2):
                        tx, tc = move(x, c)
                        tx %= 2 * nxh
                        src = (((y * nxh + x // 2) * nz + z) * 2 + x % 2) * 2 + c
                        dst = (((y * nxh + tx // 2) * nz + z) * 2 + tx % 2) * 2 + tc
                        pairs.append((src, dst))
        return lax.ppermute(value, AXES, pairs)

    swap_core = lambda v: send(v, lambda x, c: (x, 1 - c))
    swap_x = lambda v: send(v, lambda x, c: (x ^ 1, c))
    swap_x_cross = lambda v: send(v, lambda x, c: (x ^ 1, 1 - c))
    swap_out = lambda v: send(v, lambda x, c: (x ^ 3, c))
    swap_out_cross = lambda v: send(v, lambda x, c: (x ^ 3, 1 - c))
    x_plus = lambda v: send(v, lambda x, c: (x + 1, c))
    x_minus = lambda v: send(v, lambda x, c: (x - 1, c))
    x_two = lambda v: send(v, lambda x, c: (x + 2, c))

    def exchange_weight(cols_for, j, width, near):
        mine = cols_for(j)
        sister = swap_core(cols_for(j ^ 1))
        same, cross = cols_for(j ^ 2), cols_for(j ^ 3)
        pieces = [
            (j, 0, mine),
            (j ^ 1, 0, sister),
            (j ^ 2, 0, swap_x(same[:near])),
            (j ^ 3, 0, swap_x_cross(cross[:near])),
            (j ^ 2, near, swap_out(same[near:])),
            (j ^ 3, near, swap_out_cross(cross[near:])),
        ]
        out = jnp.zeros((D, width), BF16)
        for owner, offset, piece in pieces:
            out = lax.dynamic_update_slice(out, piece, (owner * SHARD + offset, 0))
        return out

    def combine(keep, received):
        return (keep.astype(F32) + received.astype(F32)).astype(BF16)

    def all_reduce_rows(keep, sent):
        chip = combine(keep, swap_core(sent))
        other = swap_x(chip)
        other = jnp.concatenate([other[ROWS:], other[:ROWS]], axis=0)
        return chip.astype(F32) + other.astype(F32)

    def reduce_rows(keep, sent):
        chip = combine(keep, swap_core(sent))
        return chip[:ROWS].astype(F32) + swap_x(chip[ROWS:]).astype(F32)

    def reorder(blocks, j):
        return jnp.concatenate(
            [lax.dynamic_index_in_dim(blocks, j ^ r, 0, keepdims=True) for r in range(4)], axis=0
        )

    def spread(pieces, j):
        rel = reorder(pieces, j)
        sister = swap_core(jnp.stack([rel[1], rel[3]]))
        far = jnp.stack([rel[2], sister[1]])
        near = jnp.stack([rel[0], sister[0]])
        a, b, t = x_plus(far), x_minus(far), x_two(near)
        got = jnp.concatenate([combine(near, t), combine(a, b)], axis=0)
        return reorder(got, j)

    def body(
        tokens, lengths, w_query, w_key, w_value, w_out, w_forget, forget_bias, norm_attn,
        w_gate, w_up, w_down, norm_ffn, cotangent,
    ):
        j = lax.axis_index("xl") * 2 + lax.axis_index("c")

        small = jnp.concatenate([norm_attn, norm_ffn, lengths[0].astype(BF16)])
        small = jnp.pad(small[None], ((0, 15), (0, D - small.shape[0])))
        packed = jnp.concatenate([tokens, small], axis=0)
        pair = jnp.stack([packed, swap_x(packed)])
        packed_all = jnp.concatenate([pair, swap_core(pair)], axis=0)
        x_rows = packed_all[:, :ROWS].reshape(4 * ROWS, D)
        small_all = packed_all[:, ROWS]
        lens = small_all[:, 2 * SHARD : 2 * SHARD + SLOTS].astype(jnp.int32)
        by_device = jnp.stack([small_all[0], small_all[2], small_all[1], small_all[3]])
        by_device = reorder(by_device, j).astype(F32)
        gain_one = by_device[:, :SHARD].reshape(1, D)
        gain_two = by_device[:, SHARD : 2 * SHARD].reshape(1, D)
        bias = jnp.pad(forget_bias.astype(F32), (0, 128 - LOCAL_HEADS))[None]

        def qkvf_for(i):
            cols = [lax.dynamic_slice_in_dim(w, i * SHARD, SHARD, 1) for w in (w_query, w_key, w_value)]
            part = lax.dynamic_slice_in_dim(w_forget, i * LOCAL_HEADS, LOCAL_HEADS, 1)
            return jnp.concatenate(cols + [jnp.pad(part, ((0, 0), (0, 128 - LOCAL_HEADS)))], axis=1)

        def gate_up_for(i):
            return jnp.concatenate(
                [lax.dynamic_slice_in_dim(w, i * FSHARD, FSHARD, 1) for w in (w_gate, w_up)], axis=1
            )

        w_qkvf = exchange_weight(qkvf_for, j, WIDTH, SHARD // 2)
        w_gate_up = exchange_weight(gate_up_for, j, 2 * FSHARD, SHARD // 3)

        cot_pair = jnp.stack([cotangent, swap_x(cotangent)])
        cot_rows = jnp.concatenate([cot_pair, swap_core(cot_pair)], axis=0).reshape(4 * ROWS, D)
        live = (jnp.arange(ROWS)[None, :] < jnp.sum(lens, axis=1, keepdims=True)).reshape(4 * ROWS, 1)
        grad_branch = jnp.where(live, cot_rows, jnp.zeros_like(cot_rows))

        keep, sent, normed, qkv, forget, probs, mixed = attention_forward(
            lens, x_rows, gain_one, w_qkvf, bias, w_out
        )
        half = x_rows[: 2 * ROWS].astype(F32)
        middle = half + all_reduce_rows(keep, sent)
        factor_two = lax.rsqrt(jnp.mean(middle * middle, axis=1, keepdims=True) + EPSILON)
        n2_half = (middle * factor_two * gain_two).astype(BF16)
        n2 = jnp.concatenate([n2_half, swap_core(n2_half)], axis=0)

        keep, sent, hidden, dgate, dup = ffn(n2, grad_branch, w_gate_up, w_down)
        incoming_two = all_reduce_rows(keep, sent)
        scaled = incoming_two * gain_two
        inner = jnp.mean(scaled * middle, axis=1, keepdims=True)
        grad_middle = grad_branch[: 2 * ROWS].astype(F32) + (
            scaled * factor_two - middle * (factor_two * factor_two * factor_two) * inner
        )
        gain_two_part = 0.5 * jnp.sum(incoming_two * middle * factor_two, axis=0)
        gab_half = grad_middle.astype(BF16)
        gab = jnp.concatenate([gab_half, swap_core(gab_half)], axis=0)

        g_down = dot(hidden, grad_branch, ATB).astype(BF16)
        g_gate = dot(n2, dgate, ATB).astype(BF16)
        g_up = dot(n2, dup, ATB).astype(BF16)
        down = dot(hidden, w_down, AB).astype(BF16)
        branch = reduce_rows(down[: 2 * ROWS], down[2 * ROWS :])
        output = jnp.where(live[:ROWS], middle[:ROWS] + branch, 0.0).astype(BF16)

        def plane_sum(parts):
            return lax.psum_scatter(parts, PLANE, scatter_dimension=0, tiled=True)

        def plane_gather(part):
            return lax.all_gather(part, PLANE, axis=0, tiled=True)

        rows_of, cols_of = SHARD // ny, FSHARD // nz

        def plane_split(g):
            g = g.reshape(4, ny, rows_of, nz, cols_of)
            return g.transpose(1, 3, 0, 2, 4).reshape(np_, 4, rows_of, cols_of)

        down_piece = plane_sum(g_down)
        down_piece = combine(down_piece, x_two(down_piece))
        gu_parts = jnp.concatenate([plane_split(g_gate), plane_split(g_up)], axis=3)
        gu_piece = plane_sum(gu_parts.reshape(np_ * 4 * rows_of, 2 * cols_of))
        gu_piece = spread(gu_piece.reshape(4, rows_of, 2 * cols_of), j)

        keep, sent, dqkvf, gain_one_part = attention_backward(
            x_rows, gain_one, gab, w_out, qkv, forget, probs, w_qkvf
        )
        own = x_rows[:ROWS].astype(F32)
        factor_one = lax.rsqrt(jnp.mean(own * own, axis=1, keepdims=True) + EPSILON)
        scaled = reduce_rows(keep, sent) * gain_one
        inner = jnp.mean(scaled * own, axis=1, keepdims=True)
        grad_tokens = grad_middle[:ROWS] + (
            scaled * factor_one - own * (factor_one * factor_one * factor_one) * inner
        )
        g_out = dot(mixed, gab, ATB).astype(BF16)
        g_qkvf = dot(normed, dqkvf, ATB)
        bias_part = jnp.sum(dqkvf[:, 3 * SHARD : 3 * SHARD + LOCAL_HEADS].astype(F32), axis=0)
        extra = jnp.concatenate(
            [
                g_qkvf[:, 3 * SHARD : 3 * SHARD + LOCAL_HEADS],
                gain_one_part.reshape(D, 1),
                gain_two_part.reshape(D, 1),
                jnp.broadcast_to(bias_part[None], (D, LOCAL_HEADS)),
            ],
            axis=1,
        )
        extra = jnp.pad(extra, ((0, 0), (0, 128 - extra.shape[1])))
        g_qkvf = jnp.concatenate([g_qkvf[:, : 3 * SHARD], extra], axis=1).astype(BF16)
        out_rows = SHARD // np_
        g_qkvf = g_qkvf.reshape(4, np_, out_rows, WIDTH).transpose(1, 0, 2, 3)
        out_piece = plane_sum(g_out)
        qkvf_piece = plane_sum(g_qkvf.reshape(D, WIDTH))
        out_piece = combine(out_piece, x_two(out_piece))
        qkvf_piece = spread(qkvf_piece.reshape(4, out_rows, WIDTH), j)

        grad_down = plane_gather(down_piece).astype(F32)
        gu = plane_gather(gu_piece.reshape(4 * rows_of, 2 * cols_of)).reshape(ny, nz, 4, rows_of, 2, cols_of)
        gu = gu.transpose(4, 0, 3, 2, 1, 5).astype(F32)
        grad_gate = gu[0].reshape(SHARD, FF)
        grad_up = gu[1].reshape(SHARD, FF)
        grad_out = plane_gather(out_piece).astype(F32)
        rows = plane_gather(qkvf_piece.reshape(4 * out_rows, WIDTH))
        rows = rows.reshape(np_, 4, out_rows, WIDTH).transpose(0, 2, 1, 3).reshape(SHARD, 4, WIDTH).astype(F32)
        grad_query = rows[:, :, :SHARD].reshape(SHARD, D)
        grad_key = rows[:, :, SHARD : 2 * SHARD].reshape(SHARD, D)
        grad_value = rows[:, :, 2 * SHARD : 3 * SHARD].reshape(SHARD, D)
        tail = rows[:, :, 3 * SHARD :]
        grad_forget = tail[:, :, :LOCAL_HEADS].reshape(SHARD, H)
        grad_norm_attn = jnp.sum(tail[:, :, LOCAL_HEADS], axis=1)
        grad_norm_ffn = jnp.sum(tail[:, :, LOCAL_HEADS + 1], axis=1)
        grad_bias = lax.dynamic_index_in_dim(tail[0], j, 0, keepdims=False)[
            LOCAL_HEADS + 2 : 2 * LOCAL_HEADS + 2
        ]
        return (
            output, grad_tokens, grad_query, grad_key, grad_value, grad_out, grad_forget, grad_bias,
            grad_norm_attn, grad_gate, grad_up, grad_down, grad_norm_ffn,
        )

    return body


SIZES = {32: (4, 2, 4), 4: (2, 2, 1)}


def solution(mesh):
    sizes = SIZES[mesh.shape["wide"]]
    ny, nxh, nz = sizes
    fine = Mesh(mesh.devices.reshape(ny, nxh, nz, 2, 2), AXES)
    rows, shard, vector = P(AXES, None), P(("xl", "c"), None), P(("xl", "c"))
    return jax.shard_map(
        make_body(sizes),
        mesh=fine,
        in_specs=(
            rows, rows, shard, shard, shard, shard, shard, vector, vector, shard, shard, shard, vector, rows,
        ),
        out_specs=(
            rows, rows, shard, shard, shard, shard, shard, vector, vector, shard, shard, shard, vector,
        ),
        check_vma=False,
    )
```

time: 2340 us -> 805 us (0.34)
  waiting for transfers between devices: 1920 us -> 471 us
  blocking collectives: 204 us -> 0 us
  matrix products: 146 us -> 20.1 us
  local copies, waits for them, and re-layouts: 30 us -> 145 us
  Pallas kernels: 0 us -> 46.8 us
  other arithmetic: 10.7 us -> 54.5 us
  starting transfers between devices: 1.1 us -> 41.5 us
    reduce_scatter x8 -> x3, waiting for transfers between devices: 951 us -> 215 us  [plane_sum(): return lax.psum_scatter(parts, PLANE, scatter_dimension=0, tiled=True)]
    psum x1 -> x0, waiting for transfers between devices: 451 us -> none  [body(): lax.psum((grad_query, grad_key, grad_value, grad_out, grad_forget, grad_b...]
    all_gather x7 -> x4, waiting for transfers between devices: 509 us -> 126 us  [plane_gather(): return lax.all_gather(part, PLANE, axis=0, tiled=True)]
    psum x1 -> x0, blocking collectives: 169 us -> none  [body(): lax.psum((grad_query, grad_key, grad_value, grad_out, grad_forget, grad_b...]
    dot_general x29 -> x6, matrix products: 146 us -> 20.1 us  [dot(): lax.dot_general(former, latter, (dims, ((), ())), preferred_element_type=...]
    ppermute x0 -> x34, waiting for transfers between devices: none -> 117 us  [send(): return lax.ppermute(value, AXES, pairs)]
    slice x0 -> x25, local copies, waits for them, and re-layouts: none -> 48.1 us  [the longest x2 24.9 us: body(): grad_up = gu[1].reshape(SHARD, FF)]
    pallas_call x0 -> x3, Pallas kernels: none -> 46.8 us  [the longest x1 20 us: ffn(): pl.pallas_call(ffn_kernel, grid=(steps,), in_specs=[pl.BlockSpec((4 * ROW...]
  transfers between devices with their start and end apart: 16 -> 42, of which waited for: 15 -> 26; matrix products, arithmetic and copies ran while one was open for 5% -> 17% of each run, Pallas kernels for 0% -> 3%
where the time goes in v1:
time: 805 us; the launch traced here: 795 us
  waiting for transfers between devices  471 us (59%)
  local copies, waits for them, and re-layouts  145 us (18%)
  other arithmetic  54.5 us (7%)
  Pallas kernels  46.8 us (6%)
  starting transfers between devices  41.5 us (5%)
  matrix products  20.1 us (2%)
  between operations  15.6 us (2%)
    reduce_scatter x3, waiting for transfers between devices, plane_sum(): return lax.psum_scatter(parts, PLANE, scatter_dimension=0, tiled=True)  215 us
    all_gather x4, waiting for transfers between devices, plane_gather(): return lax.all_gather(part, PLANE, axis=0, tiled=True)  126 us
    ppermute x34, waiting for transfers between devices, send(): return lax.ppermute(value, AXES, pairs)  117 us
    ppermute x34, starting transfers between devices, send(): return lax.ppermute(value, AXES, pairs)  40.8 us
    slice x2, local copies, waits for them, and re-layouts, body(): grad_up = gu[1].reshape(SHARD, FF)  24.9 us
    unnamed x121, local copies, waits for them, and re-layouts  23.2 us
    dot_general x6, matrix products, dot(): lax.dot_general(former, latter, (dims, ((), ())), preferred_element_type=...  20.1 us
    pallas_call x1, Pallas kernels, ffn(): pl.pallas_call(ffn_kernel, grid=(steps,), in_specs=[pl.BlockSpec((4 * ROW...  20 us
  transfers between devices with their start and end apart: 42, of which 26 were waited for; matrix products, arithmetic and copies ran while one was open for 17% of the time, Pallas kernels for 3%

profile of v1, /device:TPU:1, one launch (start us, length us, event | category | flops | bytes accessed | tf_op | source)
XLA Modules:
  0.0 794.9 jit_solution(15428776094195057783)
XLA Ops:
  23.1 3.5 constant_dynamic-slice_fusion.9
  35.4 16.9 %collective-permute-done.10 = bf16[128,1536]{1,0:T(8,128)(2,1)S(1)} collective-permute-done((bf16[128,1536]{1,0:T(8,128)(2,1)S(1)}, bf16[128,1536]{1,0:T(8,128)(2,1)S(1)}, u32[]{:S(2)}, u32[]{:S(2)}) %collective-permute-start.10) | collective-permute-done | bytes 393248 | tf_op jit(solution)/shard_map/ppermute | solution.py:339
  65.1 3.8 collective-permute-start.14
  69.7 7.3 collective-permute-done.6
  80.3 12.5 %shard_map.237 = (bf16[256,1536]{1,0:T(8,128)(2,1)S(1)}, bf16[256,1536]{1,0:T(8,128)(2,1)}, bf16[512,1536]{1,0:T(8,128)(2,1)S(1)}, bf16[512,1152]{1,0:T(8,128)(2...) custom-call(s32[4,4]{1,0:T(4,128)S(1)} %slice_convert_fusion.lens_ref, ...), custom_call_target="tpu_custom_call" | custom-call | flops 2617245696 | bytes 16777216 | tf_op jit(solution)/shard_map/pallas_call | solution.py:116
  105.6 14.4 %collective-permute-done.8 = bf16[256,1536]{1,0:T(8,128)(2,1)S(1)} collective-permute-done((bf16[256,1536]{1,0:T(8,128)(2,1)S(1)}, bf16[256,1536]{1,0:T(8,128)(2,1)S(1)}, u32[]{:S(2)}, u32[]{:S(2)}) %collective-permute-start.8) | collective-permute-done | bytes 786464 | tf_op jit(solution)/shard_map/ppermute | solution.py:339
  127.6 16.0 %collective-permute-done.16 = bf16[256,2048]{1,0:T(8,128)(2,1)S(1)} collective-permute-done((bf16[256,2048]{1,0:T(8,128)(2,1)S(1)}, bf16[256,2048]{1,0:T(8,128)(2,1)S(1)}, u32[]{:S(2)}, u32[]{:S(2)}) %collective-permute-start.16) | collective-permute-done | bytes 1048608 | tf_op jit(solution)/shard_map/ppermute | solution.py:339
  146.1 20.0 %shard_map.238 = (bf16[256,1536]{1,0:T(8,128)(2,1)S(1)}, bf16[256,1536]{1,0:T(8,128)(2,1)S(1)}, bf16[512,1024]{1,0:T(8,128)(2,1)S(1)}, bf16[512,1024]{1,0:T(8,128)(2,1)S(1)}, bf16[512,1024]{1,0:T(8,128)(2,1)S(1)}) custom-call(bf16[512,1536]{1,0:T(8,128)(2,1)} %pad_maximum_fusion.4.n2_ref, bf16[512,1536]{1,0:T(8,128)(2,1)} %bitcast_select_fusion.gb_ref, ...), custom_call_target="tpu_custom_call" | custom-call | flops 8053063680 | bytes 18874368 | tf_op jit(solution)/shard_map/pallas_call | solution.py:292
  168.9 18.7 %collective-permute-done.20 = bf16[256,1536]{1,0:T(8,128)(2,1)S(1)} collective-permute-done((bf16[256,1536]{1,0:T(8,128)(2,1)S(1)}, bf16[256,1536]{1,0:T(8,128)(2,1)S(1)}, u32[]{:S(2)}, u32[]{:S(2)}) %collective-permute-start.20) | collective-permute-done | bytes 786464 | tf_op jit(solution)/shard_map/ppermute | solution.py:339
  196.8 5.2 convolution_convert_fusion.1
  207.2 14.2 %shard_map.239 = (bf16[256,1536]{1,0:T(8,128)(2,1)S(1)}, bf16[256,1536]{1,0:T(8,128)(2,1)S(1)}, bf16[512,1280]{1,0:T(8,128)(2,1)S(1)}, f32[1,1536]{1,0:T(1,128)S(1)}) custom-call(bf16[512,1536]{1,0:T(8,128)(2,1)S(1)} %bitcast.85, f32[1,1536]{1,0:T(1,128)S(1)} %bitcast.87, bf16[512,1536]{1,0:T(8,128)(2,1)S(1)} %pad_maximum_fusion.7.gab_ref, ...), custom_call_target="tpu_custom_call" | custom-call | flops 2617245696 | bytes 16777216 | tf_op jit(solution)/shard_map/pallas_call | solution.py:220
  236.5 4.8 reshape.188
  247.1 4.8 reshape.187
  257.0 13.3 %reduce-scatter.13.cloned.1.call-done = bf16[24,1536]{1,0:T(8,128)(2,1)} async-done(((bf16[384,1536]{1,0:T(8,128)(2,1)}), bf16[24,1536]{1,0:T(8,128)(2,1)}) %reduce-scatter.13.cloned.1.call-update) | async-done | bytes 73744
  277.0 71.8 %reduce-scatter.11.cloned.1.call-done = bf16[64,1536]{1,0:T(8,128)(2,1)} async-done(((bf16[1024,1536]{1,0:T(8,128)(2,1)}), bf16[64,1536]{1,0:T(8,128)(2,1)}) %reduce-scatter.11.cloned.1.call-update) | async-done | bytes 196624 | tf_op jit(solution)/shard_map/reduce_scatter | solution.py:460
  351.5 3.5 collective-permute-done.33
  356.8 72.1 %reduce-scatter.7.cloned.1.call-done = bf16[96,1280]{1,0:T(8,128)(2,1)} async-done(((bf16[1536,1280]{1,0:T(8,128)(2,1)}), bf16[96,1280]{1,0:T(8,128)(2,1)}) %reduce-scatter.7.cloned.1.call-update) | async-done | bytes 245776 | tf_op jit(solution)/shard_map/reduce_scatter | solution.py:460
  443.0 71.1 %reduce-scatter.9.cloned.1.call-done = bf16[384,512]{1,0:T(8,128)(2,1)} async-done(((bf16[6144,512]{1,0:T(8,128)(2,1)}), bf16[384,512]{1,0:T(8,128)(2,1)}) %reduce-scatter.9.cloned.1.call-update) | async-done | bytes 393232 | tf_op jit(solution)/shard_map/reduce_scatter | solution.py:460
  526.0 4.3 collective-permute-done.32
  531.4 3.8 convolution_convert_fusion.4
  544.1 7.5 collective-permute-done.18
  552.5 7.4 collective-permute-done.23
  564.5 44.9 %all-gather.11.cloned.1.call-done = bf16[1024,1536]{1,0:T(8,128)(2,1)} async-done(((bf16[64,1536]{1,0:T(8,128)(2,1)}), bf16[1024,1536]{1,0:T(8,128)(2,1)}) %all-gather.11.cloned.1.call-update) | async-done | bytes 3145744 | tf_op jit(solution)/shard_map/all_gather | solution.py:463
  609.4 5.5 convert_element_type.273
  614.9 46.9 %all-gather.5.cloned.1.call-done = bf16[1536,1280]{1,0:T(8,128)(2,1)} async-done(((bf16[96,1280]{1,0:T(8,128)(2,1)}), bf16[1536,1280]{1,0:T(8,128)(2,1)}) %all-gather.5.cloned.1.call-update) | async-done | bytes 3932176 | tf_op jit(solution)/shard_map/all_gather | solution.py:463
  691.9 33.7 %all-gather.9.cloned.1.call-done = bf16[6144,512]{1,0:T(8,128)(2,1)} async-done(((bf16[384,512]{1,0:T(8,128)(2,1)}), bf16[6144,512]{1,0:T(8,128)(2,1)}) %all-gather.9.cloned.1.call-update) | async-done | bytes 6291472 | tf_op jit(solution)/shard_map/all_gather | solution.py:463
  725.6 13.8 %reshape.195 = f32[4,4,4,96,2,256]{5,4,3,2,1,0:T(2,128)} reshape(bf16[6144,512]{1,0:T(8,128)(2,1)} %all-gather.9.cloned.1.call-done) | data formatting | bytes 18874368 | tf_op jit(solution)/shard_map/convert_element_type | solution.py:510
  739.4 15.5 %fusion.33 = (f32[1,4,96,4,4,256]{5,0,2,3,4,1:T(1,128)}, f32[1,4,96,4,4,256]{5,0,2,3,4,1:T(1,128)S(1)}) fusion(f32[2,4,96,4,4,256]{5,0,2,3,4,1:T(2,128)} %bitcast.88), kind=kLoop, calls=%fused_computation.185 | loop fusion | bytes 25165824 | tf_op jit(solution)/shard_map/slice | solution.py:512
  754.9 6.6 copy.130
  761.5 8.5 %reshape_squeeze.6 = f32[384,4096]{1,0:T(8,128)} reshape(f32[1,4,96,4,4,256]{5,4,3,2,1,0:T(4,128)} %copy.130) | data formatting | bytes 12582912 | tf_op jit(solution)/shard_map/reshape;squeeze | solution.py:511
  770.0 9.4 %copy.131 = f32[1,4,96,4,4,256]{5,4,3,2,1,0:T(4,128)} copy(f32[1,4,96,4,4,256]{5,0,2,3,4,1:T(1,128)} %get-tuple-element.107) | data formatting | bytes 12582912 | tf_op jit(solution)/shard_map/slice | solution.py:512
  779.4 8.2 %reshape_squeeze.7 = f32[384,4096]{1,0:T(8,128)} reshape(f32[1,4,96,4,4,256]{5,4,3,2,1,0:T(4,128)} %copy.131) | data formatting | bytes 12582912 | tf_op jit(solution)/shard_map/reshape;squeeze | solution.py:512
  (322 shorter events, 189.2 us)
Async XLA Ops:
  7.2 263.2 %reduce-scatter.13.cloned.1.call-start = ((), (), s32[]{:S(2)}) async-start(), calls=%async_computation.11 | async-start | bytes 1253376
  10.5 44.1 %collective-permute-start = (bf16[144,1536]{1,0:T(8,128)(2,1)}, bf16[144,1536]{1,0:T(8,128)(2,1)S(1)}, u32[]{:S(2)}, u32[]{:S(2)}) collective-permute-start(bf16[144,1536]{1,0:T(8,128)(2,1)} %get-tuple-element.143), channel_id=1, source_target_pairs={{0,2},{1,3},{4,6},{5,7},{8,10},{9,11},{12,14},{13,15},{2,0},{3,1},... | collective-permute-start | bytes 1327112 | tf_op jit(solution)/shard_map/ppermute | solution.py:339
  16.6 39.9 %collective-permute-start.2 = (bf16[384,1280]{1,0:T(8,128)(2,1)}, bf16[384,1280]{1,0:T(8,128)(2,1)}, u32[]{:S(2)}, u32[]{:S(2)}) collective-permute-start(bf16[384,1280]{1,0:T(8,128)(2,1)} %fusion.7), channel_id=1, source_target_pairs={{0,1},{1,0},{4,5},{5,4},{8,9},{9,8},{12,13},{13,12},{2,3},{3,2},{6... | collective-permute-start | bytes 2949128 | tf_op jit(solution)/shard_map/ppermute | solution.py:339
  19.8 39.2 %collective-permute-start.3 = (bf16[192,1280]{1,0:T(8,128)(2,1)}, bf16[192,1280]{1,0:T(8,128)(2,1)}, u32[]{:S(2)}, u32[]{:S(2)}) collective-permute-start(bf16[192,1280]{1,0:T(8,128)(2,1)} %get-tuple-element.135), channel_id=1, source_target_pairs={{0,2},{1,3},{4,6},{5,7},{8,10},{9,11},{12,14},{13,15},{2,0},{3,1},... | collective-permute-start | bytes 1474568 | tf_op jit(solution)/shard_map/ppermute | solution.py:339
  21.3 39.9 %collective-permute-start.4 = (bf16[192,1280]{1,0:T(8,128)(2,1)}, bf16[192,1280]{1,0:T(8,128)(2,1)S(1)}, u32[]{:S(2)}, u32[]{:S(2)}) collective-permute-start(bf16[192,1280]{1,0:T(8,128)(2,1)} %get-tuple-element.133), channel_id=1, source_target_pairs={{0,3},{1,2},{4,7},{5,6},{8,11},{9,10},{12,15},{13,14},{2,1},{3,0},... | collective-permute-start | bytes 1474568 | tf_op jit(solution)/shard_map/ppermute | solution.py:339
  22.7 29.6 %collective-permute-start.10 = (bf16[128,1536]{1,0:T(8,128)(2,1)S(1)}, bf16[128,1536]{1,0:T(8,128)(2,1)S(1)}, u32[]{:S(2)}, u32[]{:S(2)}) collective-permute-start(bf16[128,1536]{1,0:T(8,128)(2,1)S(1)} %copy-done.41), channel_id=1, source_target_pairs={{0,2},{1,3},{4,6},{5,7},{8,10},{9,11},{12,14},{13,15},{2,0},{3,1},... | collective-permute-start | bytes 1179656 | tf_op jit(solution)/shard_map/ppermute | solution.py:339
  52.3 12.8 %collective-permute-start.5 = (bf16[192,1280]{1,0:T(8,128)(2,1)S(1)}, bf16[192,1280]{1,0:T(8,128)(2,1)S(1)}, u32[]{:S(2)}, u32[]{:S(2)}) collective-permute-start(bf16[192,1280]{1,0:T(8,128)(2,1)S(1)} %copy-done.53), channel_id=1, source_target_pairs={{0,18},{1,19},{4,22},{5,23},{8,26},{9,27},{12,30},{13,31},{2,16},{... | collective-permute-start | bytes 1474568 | tf_op jit(solution)/shard_map/ppermute | solution.py:339
  54.7 22.3 %collective-permute-start.6 = (bf16[192,1280]{1,0:T(8,128)(2,1)}, bf16[192,1280]{1,0:T(8,128)(2,1)S(1)}, u32[]{:S(2)}, u32[]{:S(2)}) collective-permute-start(bf16[192,1280]{1,0:T(8,128)(2,1)} %get-tuple-element.132), channel_id=1, source_target_pairs={{0,19},{1,18},{4,23},{5,22},{8,27},{9,26},{12,31},{13,30},{2,17},{... | collective-permute-start | bytes 1474568 | tf_op jit(solution)/shard_map/ppermute | solution.py:339
  56.5 45.8 %collective-permute-start.12 = (bf16[384,2048]{1,0:T(8,128)(2,1)}, bf16[384,2048]{1,0:T(8,128)(2,1)}, u32[]{:S(2)}, u32[]{:S(2)}) collective-permute-start(bf16[384,2048]{1,0:T(8,128)(2,1)} %pad_maximum_fusion.6), channel_id=1, source_target_pairs={{0,1},{1,0},{4,5},{5,4},{8,9},{9,8},{12,13},{13,12},{2,3},{3,2},{6... | collective-permute-start | bytes 4718600 | tf_op jit(solution)/shard_map/ppermute | solution.py:339
  59.0 18.8 %collective-permute-start.1 = (bf16[2,144,1536]{2,1,0:T(8,128)(2,1)S(1)}, bf16[2,144,1536]{2,1,0:T(8,128)(2,1)S(1)}, u32[]{:S(2)}, u32[]{:S(2)}) collective-permute-start(bf16[2,144,1536]{2,1,0:T(8,128)(2,1)S(1)} %pad_maximum_fusion.10), channel_id=1, source_target_pairs={{0,1},{1,0},{4,5},{5,4},{8,9},{9,8},{12,13},{13,12},{2,3},{3,2},{6... | collective-permute-start | bytes 2654216 | tf_op jit(solution)/shard_map/ppermute | solution.py:339
  61.2 60.4 %collective-permute-start.13 = (bf16[128,2048]{1,0:T(8,128)(2,1)}, bf16[128,2048]{1,0:T(8,128)(2,1)}, u32[]{:S(2)}, u32[]{:S(2)}) collective-permute-start(bf16[128,2048]{1,0:T(8,128)(2,1)} %pad_maximum_fusion.14), channel_id=1, source_target_pairs={{0,2},{1,3},{4,6},{5,7},{8,10},{9,11},{12,14},{13,15},{2,0},{3,1},... | collective-permute-start | bytes 1572872 | tf_op jit(solution)/shard_map/ppermute | solution.py:339
  65.1 58.3 %collective-permute-start.14 = (bf16[128,2048]{1,0:T(8,128)(2,1)}, bf16[128,2048]{1,0:T(8,128)(2,1)}, u32[]{:S(2)}, u32[]{:S(2)}) collective-permute-start(bf16[128,2048]{1,0:T(8,128)(2,1)} %pad_maximum_fusion.13), channel_id=1, source_target_pairs={{0,3},{1,2},{4,7},{5,6},{8,11},{9,10},{12,15},{13,14},{2,1},{3,0},... | collective-permute-start | bytes 1572872 | tf_op jit(solution)/shard_map/ppermute | solution.py:339
  77.0 17.8 %collective-permute-start.11 = (bf16[2,128,1536]{2,1,0:T(8,128)(2,1)S(1)}, bf16[2,128,1536]{2,1,0:T(8,128)(2,1)S(1)}, u32[]{:S(2)}, u32[]{:S(2)}) collective-permute-start(bf16[2,128,1536]{2,1,0:T(8,128)(2,1)S(1)} %pad_maximum_fusion.11), channel_id=1, source_target_pairs={{0,1},{1,0},{4,5},{5,4},{8,9},{9,8},{12,13},{13,12},{2,3},{3,2},{6... | collective-permute-start | bytes 2359304 | tf_op jit(solution)/shard_map/ppermute | solution.py:339
  92.8 6.3 collective-permute-start.7
  94.8 30.5 %collective-permute-start.15 = (bf16[256,2048]{1,0:T(8,128)(2,1)}, bf16[256,2048]{1,0:T(8,128)(2,1)}, u32[]{:S(2)}, u32[]{:S(2)}) collective-permute-start(bf16[256,2048]{1,0:T(8,128)(2,1)} %pad_maximum_fusion.9), channel_id=1, source_target_pairs={{0,18},{1,19},{4,22},{5,23},{8,26},{9,27},{12,30},{13,31},{2,16},{... | collective-permute-start | bytes 3145736 | tf_op jit(solution)/shard_map/ppermute | solution.py:339
  100.7 19.3 %collective-permute-start.8 = (bf16[256,1536]{1,0:T(8,128)(2,1)S(1)}, bf16[256,1536]{1,0:T(8,128)(2,1)S(1)}, u32[]{:S(2)}, u32[]{:S(2)}) collective-permute-start(bf16[256,1536]{1,0:T(8,128)(2,1)S(1)} %add_convert_fusion.3), channel_id=1, source_target_pairs={{0,2},{1,3},{4,6},{5,7},{8,10},{9,11},{12,14},{13,15},{2,0},{3,1},... | collective-permute-start | bytes 2359304 | tf_op jit(solution)/shard_map/ppermute | solution.py:339
  102.3 41.4 %collective-permute-start.16 = (bf16[256,2048]{1,0:T(8,128)(2,1)S(1)}, bf16[256,2048]{1,0:T(8,128)(2,1)S(1)}, u32[]{:S(2)}, u32[]{:S(2)}) collective-permute-start(bf16[256,2048]{1,0:T(8,128)(2,1)S(1)} %copy-done.48), channel_id=1, source_target_pairs={{0,19},{1,18},{4,23},{5,22},{8,27},{9,26},{12,31},{13,30},{2,17},{... | collective-permute-start | bytes 3145736 | tf_op jit(solution)/shard_map/ppermute | solution.py:339
  120.8 24.0 %collective-permute-start.9 = (bf16[256,1536]{1,0:T(8,128)(2,1)S(1)}, bf16[256,1536]{1,0:T(8,128)(2,1)S(1)}, u32[]{:S(2)}, u32[]{:S(2)}) collective-permute-start(bf16[256,1536]{1,0:T(8,128)(2,1)S(1)} %multiply_convert_fusion), channel_id=1, source_target_pairs={{0,1},{1,0},{4,5},{5,4},{8,9},{9,8},{12,13},{13,12},{2,3},{3,2},{6... | collective-permute-start | bytes 2359304 | tf_op jit(solution)/shard_map/ppermute | solution.py:339
  168.8 18.8 %collective-permute-start.20 = (bf16[256,1536]{1,0:T(8,128)(2,1)S(1)}, bf16[256,1536]{1,0:T(8,128)(2,1)S(1)}, u32[]{:S(2)}, u32[]{:S(2)}) collective-permute-start(bf16[256,1536]{1,0:T(8,128)(2,1)S(1)} %add_convert_fusion.1), channel_id=1, source_target_pairs={{0,2},{1,3},{4,6},{5,7},{8,10},{9,11},{12,14},{13,15},{2,0},{3,1},... | collective-permute-start | bytes 2359304 | tf_op jit(solution)/shard_map/ppermute | solution.py:339
  196.8 152.0 %reduce-scatter.11.cloned.1.call-start = ((), (), s32[]{:S(2)}) async-start(), calls=%async_computation.9 | async-start | bytes 3342336 | tf_op jit(solution)/shard_map/reduce_scatter | solution.py:460
  202.1 226.8 %reduce-scatter.7.cloned.1.call-start = ((), (), s32[]{:S(2)}) async-start(), calls=%async_computation.4 | async-start | bytes 4177920 | tf_op jit(solution)/shard_map/reduce_scatter | solution.py:460
  231.3 282.9 %reduce-scatter.9.cloned.1.call-start = ((), (), s32[]{:S(2)}) async-start(), calls=%async_computation.7 | async-start | bytes 6684672 | tf_op jit(solution)/shard_map/reduce_scatter | solution.py:460
  257.0 304.6 %all-gather.7.cloned.1.call-start = ((), (), s32[]{:S(2)}) async-start(), calls=%async_computation.6 | async-start | bytes 1253376 | tf_op jit(solution)/shard_map/all_gather | solution.py:463
  277.0 332.5 %all-gather.11.cloned.1.call-start = ((), (), s32[]{:S(2)}) async-start(), calls=%async_computation.10 | async-start | bytes 3342336 | tf_op jit(solution)/shard_map/all_gather | solution.py:463
  348.8 6.2 collective-permute-start.33
  356.7 305.1 %all-gather.5.cloned.1.call-start = ((), (), s32[]{:S(2)}) async-start(), calls=%async_computation.5 | async-start | bytes 4177920 | tf_op jit(solution)/shard_map/all_gather | solution.py:463
  443.0 282.6 %all-gather.9.cloned.1.call-start = ((), (), s32[]{:S(2)}) async-start(), calls=%async_computation.8 | async-start | bytes 6684672 | tf_op jit(solution)/shard_map/all_gather | solution.py:463
  518.2 7.7 collective-permute-start.30
  521.0 9.3 %collective-permute-start.32 = (bf16[2,96,512]{2,1,0:T(8,128)(2,1)S(1)}, bf16[2,96,512]{2,1,0:T(8,128)(2,1)S(1)}, u32[]{:S(2)}, u32[]{:S(2)}) collective-permute-start(bf16[2,96,512]{2,1,0:T(8,128)(2,1)S(1)} %pad_maximum_fusion.19), channel_id=1, source_target_pairs={{0,18},{1,19},{4,22},{5,23},{8,26},{9,27},{12,30},{13,31},{2,0},{3... | collective-permute-start | bytes 589832 | tf_op jit(solution)/shard_map/ppermute | solution.py:339
  522.0 8.3 %collective-permute-start.31 = (bf16[2,96,512]{2,1,0:T(8,128)(2,1)S(1)}, bf16[2,96,512]{2,1,0:T(8,128)(2,1)S(1)}, u32[]{:S(2)}, u32[]{:S(2)}) collective-permute-start(bf16[2,96,512]{2,1,0:T(8,128)(2,1)S(1)} %pad_maximum_fusion.19), channel_id=1, source_target_pairs={{0,2},{1,3},{4,6},{5,7},{8,10},{9,11},{12,14},{13,15},{2,16},{3,17... | collective-permute-start | bytes 589832 | tf_op jit(solution)/shard_map/ppermute | solution.py:339
  541.1 10.5 %collective-permute-start.18 = (bf16[128,1536]{1,0:T(8,128)(2,1)S(1)}, bf16[128,1536]{1,0:T(8,128)(2,1)S(1)}, u32[]{:S(2)}, u32[]{:S(2)}) collective-permute-start(bf16[128,1536]{1,0:T(8,128)(2,1)S(1)} %slice.259), channel_id=1, source_target_pairs={{0,2},{1,3},{4,6},{5,7},{8,10},{9,11},{12,14},{13,15},{2,0},{3,1},... | collective-permute-start | bytes 1179656 | tf_op jit(solution)/shard_map/ppermute | solution.py:339
  543.6 16.4 %collective-permute-start.23 = (bf16[128,1536]{1,0:T(8,128)(2,1)S(1)}, bf16[128,1536]{1,0:T(8,128)(2,1)S(1)}, u32[]{:S(2)}, u32[]{:S(2)}) collective-permute-start(bf16[128,1536]{1,0:T(8,128)(2,1)S(1)} %slice.265), channel_id=1, source_target_pairs={{0,2},{1,3},{4,6},{5,7},{8,10},{9,11},{12,14},{13,15},{2,0},{3,1},... | collective-permute-start | bytes 1179656 | tf_op jit(solution)/shard_map/ppermute | solution.py:339
  (66 other events, 602.6 us)
Sparse Core Ops, SparseCore 0:
  196.9 73.4 reduce-scatter.12
  273.7 75.0 reduce-scatter.10
  352.8 76.0 reduce-scatter.6
  432.7 81.3 reduce-scatter.8
  516.2 42.6 all-gather.6
  561.5 47.9 all-gather.10
  612.2 49.5 all-gather.4
  664.6 60.9 all-gather.8

commit v2 on v1

--- a/solution.py
+++ b/solution.py
@@ -321,9 +321,223 @@
     )(n2, gb, wgu, wgu, wd)
 
 
+EVEN = (0, 3, 1, 2)
+ODD = (0, 1, 3, 2)
+PARTS = (("z", EVEN), ("z", ODD), ("y", EVEN), ("y", ODD))
+STEPS = {EVEN: (1, 3), ODD: (3, 1)}
+
+
+def piece_of(part, index):
+    first, order = PARTS[part]
+    a, b = order[index // 4], order[index % 4]
+    return (b, a) if first == "z" else (a, b)
+
+
+def place(outs, part, index):
+    return outs[2 * part + index // 8], index % 8
+
+
+FUNITS = 36
+QUNITS = ((0, 4), (4, 8), (8, 12), (12, 15))
+OUNITS = ((0, 4), (4, 8), (8, 12), (12, 18))
+AUNITS = tuple(4 * (q1 - q0) + (o1 - o0) for (q0, q1), (o0, o1) in zip(QUNITS, OUNITS))
+NQ, NO = 240, 288
+
+
+def ffn_grad_kernel(at_ref, n2_ref, gb_ref, hidden_ref, dg_ref, du_ref, *rest):
+    outs, (gate_ref, up_ref, down_ref) = rest[:8], rest[8:]
+    y, z, j = at_ref[0], at_ref[1], at_ref[2]
+    n2 = n2_ref[...]
+    for rz in range(4):
+        lanes = pl.ds(pl.multiple_of((rz ^ z) * FBLOCK, FBLOCK), FBLOCK)
+        gate_ref[...] = dot(n2, dg_ref[:, lanes], ATB).astype(BF16).reshape(16, 96, FBLOCK)
+        up_ref[...] = dot(n2, du_ref[:, lanes], ATB).astype(BF16).reshape(16, 96, FBLOCK)
+        down_ref[...] = dot(hidden_ref[:, lanes], gb_ref[...], ATB).astype(BF16).reshape(4, 64, D)
+        for part in range(4):
+            source = (gate_ref, gate_ref, up_ref, up_ref)[part]
+            left = part % 2 * 128
+            for index in range(16):
+                ry, own_rz = piece_of(part, index)
+                if own_rz != rz:
+                    continue
+                out, slot = place(outs, part, index)
+                py = ry ^ y
+                for r in range(4):
+                    block = source[(r ^ j) * 4 + py, :, left : left + 128]
+                    out[slot, 6 * r : 6 * r + 6] = block.reshape(6, 16, 128)
+                for t in range(3):
+                    lane = 384 * part + 128 * t
+                    block = down_ref[py, :, lane : lane + 128]
+                    out[slot, 24 + 4 * t : 28 + 4 * t] = block.reshape(4, 16, 128)
+
+
+def ffn_gradients(at, n2, gb, hidden, dg, du):
+    vmem = pl.BlockSpec(memory_space=pltpu.VMEM)
+    return pl.pallas_call(
+        ffn_grad_kernel,
+        in_specs=[pl.BlockSpec(memory_space=pltpu.SMEM)] + [vmem] * 5,
+        out_specs=[vmem] * 8,
+        out_shape=[jax.ShapeDtypeStruct((8, FUNITS, 16, 128), BF16)] * 8,
+        scratch_shapes=[
+            pltpu.VMEM((16, 96, FBLOCK), BF16),
+            pltpu.VMEM((16, 96, FBLOCK), BF16),
+            pltpu.VMEM((4, 64, D), BF16),
+        ],
+        compiler_params=pltpu.CompilerParams(vmem_limit_bytes=48 * 1024 * 1024),
+        cost_estimate=pl.CostEstimate(
+            flops=2 * 4 * ROWS * D * FSHARD * 3, bytes_accessed=16 * 1024 * 1024, transcendentals=0
+        ),
+    )(at, n2, gb, hidden, dg, du)
+
+
+def ffn_unpack_kernel(at_ref, *refs):
+    ins, (gate_ref, up_ref, down_ref) = refs[:8], refs[8:]
+    y, z, j = at_ref[0], at_ref[1], at_ref[2]
+    for part in range(4):
+        target = (gate_ref, gate_ref, up_ref, up_ref)[part]
+        for index in range(16):
+            ry, rz = piece_of(part, index)
+            source, slot = place(ins, part, index)
+            py, pz = ry ^ y, rz ^ z
+            rows = pl.ds(pl.multiple_of(py * 96, 32), 96)
+            for r in range(4):
+                left = (r ^ j) * FSHARD + pz * FBLOCK + part % 2 * 128
+                block = source[slot, 6 * r : 6 * r + 6].reshape(96, 128)
+                target[rows, pl.ds(pl.multiple_of(left, 128), 128)] = block.astype(F32)
+            rows = pl.ds(pl.multiple_of(pz * 256 + py * 64, 64), 64)
+            for t in range(3):
+                left = 384 * part + 128 * t
+                block = source[slot, 24 + 4 * t : 28 + 4 * t].reshape(64, 128)
+                down_ref[rows, left : left + 128] = block.astype(F32)
+
+
+def ffn_unpack(at, pieces):
+    vmem = pl.BlockSpec(memory_space=pltpu.VMEM)
+    return pl.pallas_call(
+        ffn_unpack_kernel,
+        in_specs=[pl.BlockSpec(memory_space=pltpu.SMEM)] + [vmem] * 8,
+        out_specs=[vmem] * 3,
+        out_shape=[
+            jax.ShapeDtypeStruct((SHARD, FF), F32),
+            jax.ShapeDtypeStruct((SHARD, FF), F32),
+            jax.ShapeDtypeStruct((FSHARD, D), F32),
+        ],
+        compiler_params=pltpu.CompilerParams(vmem_limit_bytes=48 * 1024 * 1024),
+        cost_estimate=pl.CostEstimate(flops=0, bytes_accessed=28 * 1024 * 1024, transcendentals=0),
+    )(at, *pieces)
+
+
+def attention_grad_kernel(at_ref, normed_ref, dqkvf_ref, mixed_ref, gab_ref, gains_ref, *rest):
+    outs, (q_ref, o_ref) = rest[:8], rest[8:]
+    y, z, j = at_ref[0], at_ref[1], at_ref[2]
+    dqkvf = dqkvf_ref[...]
+    row = lax.broadcasted_iota(jnp.int32, (16, 128), 0)
+    lane = lax.broadcasted_iota(jnp.int32, (16, 128), 1)
+    pick = (lane == row + LOCAL_HEADS).astype(BF16)
+    pick = jnp.where(row < 2, pick, jnp.zeros_like(pick))
+    bias = jnp.sum(dqkvf[:, 3 * SHARD :].astype(F32), axis=0, keepdims=True)
+    bias = pltpu.roll(bias, 8, 1)
+    pieces = [[piece_of(part, index) for index in range(16)] for part in range(4)]
+    for r in range(4):
+        lanes = pl.ds(pl.multiple_of((r ^ j) * SHARD, SHARD), SHARD)
+        grad = dot(normed_ref[:, lanes], dqkvf, ATB)
+        extra = grad[:, 3 * SHARD :] + dot(gains_ref[:, lanes], pick, ATB) + bias
+        for col in range(9):
+            block = grad[:, 128 * col : 128 * col + 128].astype(BF16).reshape(24, 1, 16, 128)
+            q_ref[:, col : col + 1] = block
+        q_ref[:, 9:10] = extra.astype(BF16).reshape(24, 1, 16, 128)
+        for part in range(4):
+            lo, hi = QUNITS[part]
+            for index in range(16):
+                ry, rz = pieces[part][index]
+                out, slot = place(outs, part, index)
+                p = (ry ^ y) * 4 + (rz ^ z)
+                odd = p & 1
+                base = (p >> 1) * 3
+                for t in range(lo, hi):
+                    group = base + jnp.where(odd == 1, (15 + t) // 10, t // 10)
+                    col = jnp.where(odd == 1, (15 + t) % 10, t % 10)
+                    out[slot, (hi - lo) * r + t - lo] = q_ref[group, col]
+    grad = dot(mixed_ref[...], gab_ref[...], ATB)
+    for col in range(12):
+        o_ref[:, col : col + 1] = grad[:, 128 * col : 128 * col + 128].astype(BF16).reshape(24, 1, 16, 128)
+    for part in range(4):
+        lo, hi = OUNITS[part]
+        first = AUNITS[part] - (hi - lo)
+        for index in range(16):
+            ry, rz = pieces[part][index]
+            out, slot = place(outs, part, index)
+            p = (ry ^ y) * 4 + (rz ^ z)
+            odd = p & 1
+            base = (p >> 1) * 3
+            for t in range(lo, hi):
+                group = base + jnp.where(odd == 1, (18 + t) // 12, t // 12)
+                col = jnp.where(odd == 1, (18 + t) % 12, t % 12)
+                out[slot, first + t - lo] = o_ref[group, col]
+
+
+def attention_gradients(at, normed, dqkvf, mixed, gab, gains):
+    vmem = pl.BlockSpec(memory_space=pltpu.VMEM)
+    return pl.pallas_call(
+        attention_grad_kernel,
+        in_specs=[pl.BlockSpec(memory_space=pltpu.SMEM)] + [vmem] * 5,
+        out_specs=[vmem] * 8,
+        out_shape=[jax.ShapeDtypeStruct((8, AUNITS[i // 2], 16, 128), BF16) for i in range(8)],
+        scratch_shapes=[
+            pltpu.VMEM((24, 10, 16, 128), BF16),
+            pltpu.VMEM((24, 12, 16, 128), BF16),
+        ],
+        compiler_params=pltpu.CompilerParams(vmem_limit_bytes=48 * 1024 * 1024),
+        cost_estimate=pl.CostEstimate(
+            flops=2 * 4 * ROWS * D * (WIDTH + SHARD), bytes_accessed=10 * 1024 * 1024, transcendentals=0
+        ),
+    )(at, normed, dqkvf, mixed, gab, gains)
+
+
+def attention_unpack_kernel(at_ref, *refs):
+    ins, (gq_ref, gk_ref, gv_ref, go_ref, extra_ref, q_ref, o_ref) = refs[:8], refs[8:]
+    y, z, j = at_ref[0], at_ref[1], at_ref[2]
+    for part in range(4):
+        qlo, qhi = QUNITS[part]
+        olo, ohi = OUNITS[part]
+        for index in range(16):
+            ry, rz = piece_of(part, index)
+            source, slot = place(ins, part, index)
+            p = (ry ^ y) * 4 + (rz ^ z)
+            n = qhi - qlo
+            for r in range(4):
+                q_ref[r ^ j, pl.ds(p * 15 + qlo, n)] = source[slot, n * r : n * r + n]
+            o_ref[pl.ds(p * 18 + olo, ohi - olo)] = source[slot, 4 * n : 4 * n + ohi - olo]
+    for group in range(24):
+        rows = slice(16 * group, 16 * group + 16)
+        for device in range(4):
+            for col in range(10):
+                value = q_ref[device, 10 * group + col].astype(F32)
+                target = (gq_ref, gk_ref, gv_ref, extra_ref)[col // 3]
+                left = 128 * device if col == 9 else SHARD * device + 128 * (col % 3)
+                target[rows, left : left + 128] = value
+        for col in range(12):
+            go_ref[rows, 128 * col : 128 * col + 128] = o_ref[12 * group + col].astype(F32)
+
+
+def attention_unpack(at, pieces):
+    vmem = pl.BlockSpec(memory_space=pltpu.VMEM)
+    return pl.pallas_call(
+        attention_unpack_kernel,
+        in_specs=[pl.BlockSpec(memory_space=pltpu.SMEM)] + [vmem] * 8,
+        out_specs=[vmem] * 5,
+        out_shape=[jax.ShapeDtypeStruct((SHARD, D), F32)] * 4 + [jax.ShapeDtypeStruct((SHARD, 512), F32)],
+        scratch_shapes=[
+            pltpu.VMEM((4, NQ, 16, 128), BF16),
+            pltpu.VMEM((NO, 16, 128), BF16),
+        ],
+        compiler_params=pltpu.CompilerParams(vmem_limit_bytes=48 * 1024 * 1024),
+        cost_estimate=pl.CostEstimate(flops=0, bytes_accessed=16 * 1024 * 1024, transcendentals=0),
+    )(at, *pieces)
+
+
 def make_body(sizes):
     ny, nxh, nz = sizes
-    np_ = ny * nz
 
     def send(value, move):
         pairs = []
@@ -331,41 +545,48 @@
             for x in range(2 * nxh):
                 for z in range(nz):
                     for c in range(2):
-                        tx, tc = move(x, c)
+                        ty, tx, tz, tc = move(y, x, z, c)
                         tx %= 2 * nxh
                         src = (((y * nxh + x // 2) * nz + z) * 2 + x % 2) * 2 + c
-                        dst = (((y * nxh + tx // 2) * nz + z) * 2 + tx % 2) * 2 + tc
+                        dst = (((ty * nxh + tx // 2) * nz + tz) * 2 + tx % 2) * 2 + tc
                         pairs.append((src, dst))
         return lax.ppermute(value, AXES, pairs)
 
-    swap_core = lambda v: send(v, lambda x, c: (x, 1 - c))
-    swap_x = lambda v: send(v, lambda x, c: (x ^ 1, c))
-    swap_x_cross = lambda v: send(v, lambda x, c: (x ^ 1, 1 - c))
-    swap_out = lambda v: send(v, lambda x, c: (x ^ 3, c))
-    swap_out_cross = lambda v: send(v, lambda x, c: (x ^ 3, 1 - c))
-    x_plus = lambda v: send(v, lambda x, c: (x + 1, c))
-    x_minus = lambda v: send(v, lambda x, c: (x - 1, c))
-    x_two = lambda v: send(v, lambda x, c: (x + 2, c))
+    def swap_plane(value, axis, bits):
+        if axis == "y":
+            return send(value, lambda y, x, z, c: (y ^ bits, x, z, c))
+        return send(value, lambda y, x, z, c: (y, x, z ^ bits, c))
+
+    swap_core = lambda v: send(v, lambda y, x, z, c: (y, x, z, 1 - c))
+    swap_x = lambda v: send(v, lambda y, x, z, c: (y, x ^ 1, z, c))
+    swap_out = lambda v: send(v, lambda y, x, z, c: (y, x ^ 3, z, c))
+    x_plus = lambda v: send(v, lambda y, x, z, c: (y, x + 1, z, c))
+    x_minus = lambda v: send(v, lambda y, x, z, c: (y, x - 1, z, c))
+    x_two = lambda v: send(v, lambda y, x, z, c: (y, x + 2, z, c))
 
     def exchange_weight(cols_for, j, width, near):
-        mine = cols_for(j)
+        far = jnp.concatenate([cols_for(j ^ 2), cols_for(j ^ 3)], axis=1)
+        inner, outer = swap_x(far[:near]), swap_out(far[near:])
         sister = swap_core(cols_for(j ^ 1))
-        same, cross = cols_for(j ^ 2), cols_for(j ^ 3)
+        cross_inner, cross_outer = swap_core(inner[:, width:]), swap_core(outer[:, width:])
         pieces = [
-            (j, 0, mine),
+            (j, 0, cols_for(j)),
             (j ^ 1, 0, sister),
-            (j ^ 2, 0, swap_x(same[:near])),
-            (j ^ 3, 0, swap_x_cross(cross[:near])),
-            (j ^ 2, near, swap_out(same[near:])),
-            (j ^ 3, near, swap_out_cross(cross[near:])),
+            (j ^ 2, 0, inner[:, :width]),
+            (j ^ 2, near, outer[:, :width]),
+            (j ^ 3, 0, cross_inner),
+            (j ^ 3, near, cross_outer),
         ]
         out = jnp.zeros((D, width), BF16)
         for owner, offset, piece in pieces:
             out = lax.dynamic_update_slice(out, piece, (owner * SHARD + offset, 0))
         return out
 
+    def total(parts):
+        return functools.reduce(lambda a, b: a + b, [p.astype(F32) for p in parts])
+
     def combine(keep, received):
-        return (keep.astype(F32) + received.astype(F32)).astype(BF16)
+        return total([keep, received]).astype(BF16)
 
     def all_reduce_rows(keep, sent):
         chip = combine(keep, swap_core(sent))
@@ -377,25 +598,55 @@
         chip = combine(keep, swap_core(sent))
         return chip[:ROWS].astype(F32) + swap_x(chip[ROWS:]).astype(F32)
 
-    def reorder(blocks, j):
-        return jnp.concatenate(
-            [lax.dynamic_index_in_dim(blocks, j ^ r, 0, keepdims=True) for r in range(4)], axis=0
-        )
-
-    def spread(pieces, j):
-        rel = reorder(pieces, j)
-        sister = swap_core(jnp.stack([rel[1], rel[3]]))
-        far = jnp.stack([rel[2], sister[1]])
-        near = jnp.stack([rel[0], sister[0]])
+    def moves(part):
+        first, order = PARTS[part]
+        second = "y" if first == "z" else "z"
+        return [(axis, bits) for axis in (first, second) for bits in STEPS[order]]
+
+    def plane_sum(parts):
+        held = [[parts[2 * k]] for k in range(4)]
+        sending = [parts[2 * k + 1] for k in range(4)]
+        for step in range(4):
+            half = 4 >> step
+            for k in range(4):
+                axis, bits = moves(k)[step]
+                held[k].append(swap_plane(sending[k], axis, bits))
+            for k in range(4):
+                if half:
+                    sending[k] = total([h[half : 2 * half] for h in held[k]]).astype(BF16)
+        return [total([h[:1] for h in held[k]]).astype(BF16)[0] for k in range(4)]
+
+    def plane_gather(pieces):
+        out = [p[None] for p in pieces]
+        for step in (3, 2, 1, 0):
+            got = [swap_plane(out[k], *moves(k)[step]) for k in range(4)]
+            if step:
+                out = [jnp.concatenate([out[k], got[k]], axis=0) for k in range(4)]
+        return [v for k in range(4) for v in (out[k], got[k])]
+
+    def spread(pieces, columns):
+        rel = [p[: 4 * n].reshape(4, n, 16, 128) for p, n in zip(pieces, columns)]
+        own = [p[4 * n :] for p, n in zip(pieces, columns)]
+        sister = swap_core(jnp.concatenate([r[i] for i in (1, 3) for r in rel], axis=0))
+        n = sum(columns)
+        far = jnp.concatenate([r[2] for r in rel] + [sister[n:]], axis=0)
+        near = jnp.concatenate([r[0] for r in rel] + [sister[:n]] + own, axis=0)
         a, b, t = x_plus(far), x_minus(far), x_two(near)
-        got = jnp.concatenate([combine(near, t), combine(a, b)], axis=0)
-        return reorder(got, j)
+        near, far = combine(near, t), combine(a, b)
+        out, at, tail = [], 0, 2 * n
+        for p, m in zip(pieces, columns):
+            last = p.shape[0] - 4 * m
+            blocks = [v[lo + at : lo + at + m] for v in (near, far) for lo in (0, n)]
+            out.append(jnp.concatenate(blocks + [near[tail : tail + last]], axis=0))
+            at, tail = at + m, tail + last
+        return out
 
     def body(
         tokens, lengths, w_query, w_key, w_value, w_out, w_forget, forget_bias, norm_attn,
         w_gate, w_up, w_down, norm_ffn, cotangent,
     ):
         j = lax.axis_index("xl") * 2 + lax.axis_index("c")
+        at = jnp.stack([lax.axis_index("y"), lax.axis_index("z"), j]).astype(jnp.int32)
 
         small = jnp.concatenate([norm_attn, norm_ffn, lengths[0].astype(BF16)])
         small = jnp.pad(small[None], ((0, 15), (0, D - small.shape[0])))
@@ -406,7 +657,9 @@
         small_all = packed_all[:, ROWS]
         lens = small_all[:, 2 * SHARD : 2 * SHARD + SLOTS].astype(jnp.int32)
         by_device = jnp.stack([small_all[0], small_all[2], small_all[1], small_all[3]])
-        by_device = reorder(by_device, j).astype(F32)
+        by_device = jnp.concatenate(
+            [lax.dynamic_index_in_dim(by_device, j ^ r, 0, keepdims=True) for r in range(4)], axis=0
+        ).astype(F32)
         gain_one = by_device[:, :SHARD].reshape(1, D)
         gain_two = by_device[:, SHARD : 2 * SHARD].reshape(1, D)
         bias = jnp.pad(forget_bias.astype(F32), (0, 128 - LOCAL_HEADS))[None]
@@ -421,7 +674,7 @@
                 [lax.dynamic_slice_in_dim(w, i * FSHARD, FSHARD, 1) for w in (w_gate, w_up)], axis=1
             )
 
-        w_qkvf = exchange_weight(qkvf_for, j, WIDTH, SHARD // 2)
+        w_qkvf = exchange_weight(qkvf_for, j, WIDTH, 144)
         w_gate_up = exchange_weight(gate_up_for, j, 2 * FSHARD, SHARD // 3)
 
         cot_pair = jnp.stack([cotangent, swap_x(cotangent)])
@@ -449,34 +702,21 @@
         gab_half = grad_middle.astype(BF16)
         gab = jnp.concatenate([gab_half, swap_core(gab_half)], axis=0)
 
-        g_down = dot(hidden, grad_branch, ATB).astype(BF16)
-        g_gate = dot(n2, dgate, ATB).astype(BF16)
-        g_up = dot(n2, dup, ATB).astype(BF16)
+        ffn_pieces = plane_sum(ffn_gradients(at, n2, grad_branch, hidden, dgate, dup))
+        ffn_pieces = spread(ffn_pieces, [6] * 4)
+
         down = dot(hidden, w_down, AB).astype(BF16)
         branch = reduce_rows(down[: 2 * ROWS], down[2 * ROWS :])
         output = jnp.where(live[:ROWS], middle[:ROWS] + branch, 0.0).astype(BF16)
 
-        def plane_sum(parts):
-            return lax.psum_scatter(parts, PLANE, scatter_dimension=0, tiled=True)
-
-        def plane_gather(part):
-            return lax.all_gather(part, PLANE, axis=0, tiled=True)
-
-        rows_of, cols_of = SHARD // ny, FSHARD // nz
-
-        def plane_split(g):
-            g = g.reshape(4, ny, rows_of, nz, cols_of)
-            return g.transpose(1, 3, 0, 2, 4).reshape(np_, 4, rows_of, cols_of)
-
-        down_piece = plane_sum(g_down)
-        down_piece = combine(down_piece, x_two(down_piece))
-        gu_parts = jnp.concatenate([plane_split(g_gate), plane_split(g_up)], axis=3)
-        gu_piece = plane_sum(gu_parts.reshape(np_ * 4 * rows_of, 2 * cols_of))
-        gu_piece = spread(gu_piece.reshape(4, rows_of, 2 * cols_of), j)
-
         keep, sent, dqkvf, gain_one_part = attention_backward(
             x_rows, gain_one, gab, w_out, qkv, forget, probs, w_qkvf
         )
+        gains = jnp.concatenate([gain_one_part, gain_two_part[None]], axis=0).astype(BF16)
+        gains = jnp.pad(gains, ((0, 14), (0, 0)))
+        attn_pieces = plane_sum(attention_gradients(at, normed, dqkvf, mixed, gab, gains))
+        attn_pieces = spread(attn_pieces, [hi - lo for lo, hi in QUNITS])
+
         own = x_rows[:ROWS].astype(F32)
         factor_one = lax.rsqrt(jnp.mean(own * own, axis=1, keepdims=True) + EPSILON)
         scaled = reduce_rows(keep, sent) * gain_one
@@ -484,45 +724,14 @@
         grad_tokens = grad_middle[:ROWS] + (
             scaled * factor_one - own * (factor_one * factor_one * factor_one) * inner
         )
-        g_out = dot(mixed, gab, ATB).astype(BF16)
-        g_qkvf = dot(normed, dqkvf, ATB)
-        bias_part = jnp.sum(dqkvf[:, 3 * SHARD : 3 * SHARD + LOCAL_HEADS].astype(F32), axis=0)
-        extra = jnp.concatenate(
-            [
-                g_qkvf[:, 3 * SHARD : 3 * SHARD + LOCAL_HEADS],
-                gain_one_part.reshape(D, 1),
-                gain_two_part.reshape(D, 1),
-                jnp.broadcast_to(bias_part[None], (D, LOCAL_HEADS)),
-            ],
-            axis=1,
-        )
-        extra = jnp.pad(extra, ((0, 0), (0, 128 - extra.shape[1])))
-        g_qkvf = jnp.concatenate([g_qkvf[:, : 3 * SHARD], extra], axis=1).astype(BF16)
-        out_rows = SHARD // np_
-        g_qkvf = g_qkvf.reshape(4, np_, out_rows, WIDTH).transpose(1, 0, 2, 3)
-        out_piece = plane_sum(g_out)
-        qkvf_piece = plane_sum(g_qkvf.reshape(D, WIDTH))
-        out_piece = combine(out_piece, x_two(out_piece))
-        qkvf_piece = spread(qkvf_piece.reshape(4, out_rows, WIDTH), j)
-
-        grad_down = plane_gather(down_piece).astype(F32)
-        gu = plane_gather(gu_piece.reshape(4 * rows_of, 2 * cols_of)).reshape(ny, nz, 4, rows_of, 2, cols_of)
-        gu = gu.transpose(4, 0, 3, 2, 1, 5).astype(F32)
-        grad_gate = gu[0].reshape(SHARD, FF)
-        grad_up = gu[1].reshape(SHARD, FF)
-        grad_out = plane_gather(out_piece).astype(F32)
-        rows = plane_gather(qkvf_piece.reshape(4 * out_rows, WIDTH))
-        rows = rows.reshape(np_, 4, out_rows, WIDTH).transpose(0, 2, 1, 3).reshape(SHARD, 4, WIDTH).astype(F32)
-        grad_query = rows[:, :, :SHARD].reshape(SHARD, D)
-        grad_key = rows[:, :, SHARD : 2 * SHARD].reshape(SHARD, D)
-        grad_value = rows[:, :, 2 * SHARD : 3 * SHARD].reshape(SHARD, D)
-        tail = rows[:, :, 3 * SHARD :]
-        grad_forget = tail[:, :, :LOCAL_HEADS].reshape(SHARD, H)
-        grad_norm_attn = jnp.sum(tail[:, :, LOCAL_HEADS], axis=1)
-        grad_norm_ffn = jnp.sum(tail[:, :, LOCAL_HEADS + 1], axis=1)
-        grad_bias = lax.dynamic_index_in_dim(tail[0], j, 0, keepdims=False)[
-            LOCAL_HEADS + 2 : 2 * LOCAL_HEADS + 2
-        ]
+
+        grad_gate, grad_up, grad_down = ffn_unpack(at, plane_gather(ffn_pieces))
+        grad_query, grad_key, grad_value, grad_out, extra = attention_unpack(at, plane_gather(attn_pieces))
+        extra = extra.reshape(SHARD, 4, 128)
+        grad_forget = extra[:, :, :LOCAL_HEADS].reshape(SHARD, H)
+        grad_norm_attn = jnp.sum(extra[:, :, LOCAL_HEADS], axis=1)
+        grad_norm_ffn = jnp.sum(extra[:, :, LOCAL_HEADS + 1], axis=1)
+        grad_bias = lax.dynamic_index_in_dim(extra[0], j, 0, keepdims=False)[8 : 8 + LOCAL_HEADS]
         return (
             output, grad_tokens, grad_query, grad_key, grad_value, grad_out, grad_forget, grad_bias,
             grad_norm_attn, grad_gate, grad_up, grad_down, grad_norm_ffn,
@@ -531,7 +740,7 @@
     return body
 
 
-SIZES = {32: (4, 2, 4), 4: (2, 2, 1)}
+SIZES = {32: (4, 2, 4), 16: (4, 1, 4)}
 
 
 def solution(mesh):

time: 805 us -> 491 us (0.61)
  the two profiles are of different devices: /device:TPU:1 before, /device:TPU:10 now
where the time goes in v2:
time: 491 us; the launch traced here: 481 us
  waiting for transfers between devices  192 us (39%)
  starting transfers between devices  124 us (25%)
  Pallas kernels  79.4 us (16%)
  local copies, waits for them, and re-layouts  45 us (9%)
  other arithmetic  34.3 us (7%)
    ppermute x96, waiting for transfers between devices, send(): return lax.ppermute(value, AXES, pairs)  192 us
    ppermute x96, starting transfers between devices, send(): return lax.ppermute(value, AXES, pairs)  124 us
    pallas_call x1, Pallas kernels, ffn(): pl.pallas_call(ffn_kernel, grid=(steps,), in_specs=[pl.BlockSpec((4 * ROW...  20 us
    unnamed x122, local copies, waits for them, and re-layouts  18.9 us
    pallas_call x1, Pallas kernels, attention_backward(): pl.pallas_call(backward_kernel, grid=(4,), in_specs=[pl.BlockSpec((ROWS,...  14.2 us
    pallas_call x1, Pallas kernels, attention_forward(): pl.pallas_call(forward_kernel, grid=(4,), in_specs=[pl.BlockSpec(memory_s...  12.5 us
    pallas_call x1, Pallas kernels, ffn_gradients(): pl.pallas_call(ffn_grad_kernel, in_specs=[pl.BlockSpec(memory_space=pltpu...  10.8 us
    pallas_call x1, Pallas kernels, ffn_unpack(): pl.pallas_call(ffn_unpack_kernel, in_specs=[pl.BlockSpec(memory_space=plt...  10.7 us
  transfers between devices with their start and end apart: 96, of which 34 were waited for; matrix products, arithmetic and copies ran while one was open for 14% of the time, Pallas kernels for 11%

profile of v2, /device:TPU:10, one launch (start us, length us, event | category | flops | bytes accessed | tf_op | source)
XLA Modules:
  0.0 481.5 jit_solution(3138772710818317881)
XLA Ops:
  39.5 7.1 %collective-permute-done.4 = bf16[240,2560]{1,0:T(8,128)(2,1)S(1)} collective-permute-done((bf16[240,2560]{1,0:T(8,128)(2,1)}, bf16[240,2560]{1,0:T(8,128)(2,1)S(1)}, u32[]{:S(2)}, u32[]{:S(2)}) %collective-permute-start.4) | collective-permute-done | bytes 1228832 | tf_op jit(solution)/shard_map/ppermute | solution.py:553
  50.2 12.5 %shard_map.237 = (bf16[256,1536]{1,0:T(8,128)(2,1)S(1)}, bf16[256,1536]{1,0:T(8,128)(2,1)}, bf16[512,1536]{1,0:T(8,128)(2,1)S(1)}, bf16[512,1152]{1,0:T(8,128)(2...) custom-call(s32[4,4]{1,0:T(4,128)S(1)} %slice_convert_fusion.lens_ref, ...), custom_call_target="tpu_custom_call" | custom-call | flops 2617245696 | bytes 16777216 | tf_op jit(solution)/shard_map/pallas_call | solution.py:116
  74.9 21.4 %collective-permute-done.14 = bf16[256,4096]{1,0:T(8,128)(2,1)} collective-permute-done((bf16[256,4096]{1,0:T(8,128)(2,1)}, bf16[256,4096]{1,0:T(8,128)(2,1)}, u32[]{:S(2)}, u32[]{:S(2)}) %collective-permute-start.14) | collective-permute-done | bytes 2097184 | tf_op jit(solution)/shard_map/ppermute | solution.py:553
  106.6 20.0 %shard_map.238 = (bf16[256,1536]{1,0:T(8,128)(2,1)S(1)}, bf16[256,1536]{1,0:T(8,128)(2,1)S(1)}, bf16[512,1024]{1,0:T(8,128)(2,1)S(1)}, bf16[512,1024]{1,0:T(8,128)(2,1)S(1)}, bf16[512,1024]{1,0:T(8,128)(2,1)S(1)}) custom-call(bf16[512,1536]{1,0:T(8,128)(2,1)} %pad_maximum_fusion.5.n2_ref, bf16[512,1536]{1,0:T(8,128)(2,1)} %bitcast_select_fusion.gb_ref, ...), custom_call_target="tpu_custom_call" | custom-call | flops 8053063680 | bytes 18874368 | tf_op jit(solution)/shard_map/pallas_call | solution.py:292
  131.0 10.8 %shard_map.242 = (bf16[8,36,16,128]{3,2,1,0:T(8,128)(2,1)S(1)}, bf16[8,36,16,128]{3,2,1,0:T(8,128)(2,1)S(1)}, bf16[8,36,16,128]{3,2,1,0:T(8,128)(2,1)}, bf16[8,3...) custom-call(s32[3]{0:T(128)S(1)} %pad_add_fusion.at_ref, ...), custom_call_target="tpu_custom_call" | custom-call | flops 4831838208 | bytes 16777216 | tf_op jit(solution)/shard_map/pallas_call | solution.py:376
  157.5 13.3 %collective-permute-done.60 = bf16[8,36,16,128]{3,2,1,0:T(8,128)(2,1)S(1)} collective-permute-done((bf16[8,36,16,128]{3,2,1,0:T(8,128)(2,1)S(1)}, bf16[8,36,16,128]{3,2,1,0:T(8,128)(2,1)S(1)}, u32[]{:S(2)}, u32[]{:S(2)}) %collective-permute-start.60) | collective-permute-done | bytes 1179680 | tf_op jit(solution)/shard_map/ppermute | solution.py:553
  174.5 4.0 collective-permute-start.61
  186.0 5.4 %collective-permute-done.61 = bf16[4,36,16,128]{3,2,1,0:T(8,128)(2,1)S(1)} collective-permute-done((bf16[4,36,16,128]{3,2,1,0:T(8,128)(2,1)S(1)}, bf16[4,36,16,128]{3,2,1,0:T(8,128)(2,1)S(1)}, u32[]{:S(2)}, u32[]{:S(2)}) %collective-permute-start.61) | collective-permute-done | bytes 589856 | tf_op jit(solution)/shard_map/ppermute | solution.py:553
  221.8 14.2 %shard_map.239 = (bf16[256,1536]{1,0:T(8,128)(2,1)S(1)}, bf16[256,1536]{1,0:T(8,128)(2,1)S(1)}, bf16[512,1280]{1,0:T(8,128)(2,1)S(1)}, f32[1,1536]{1,0:T(1,128)S(1)}) custom-call(bf16[512,1536]{1,0:T(8,128)(2,1)S(1)} %bitcast.224, f32[1,1536]{1,0:T(1,128)S(1)} %bitcast.226, bf16[512,1536]{1,0:T(8,128)(2,1)S(1)} %pad_maximum_fusion.8.gab_ref, ...), custom_call_target="tpu_custom_call" | custom-call | flops 2617245696 | bytes 16777216 | tf_op jit(solution)/shard_map/pallas_call | solution.py:220
  245.9 6.5 %shard_map.240 = (bf16[8,20,16,128]{3,2,1,0:T(8,128)(2,1)S(1)}, bf16[8,20,16,128]{3,2,1,0:T(8,128)(2,1)S(1)}, bf16[8,20,16,128]{3,2,1,0:T(8,128)(2,1)S(1)}, bf16...) custom-call(s32[3]{0:T(128)S(1)} %pad_add_fusion.at_ref, ...), custom_call_target="tpu_custom_call" | custom-call | flops 2617245696 | bytes 10485760 | tf_op jit(solution)/shard_map/pallas_call | solution.py:481
  262.6 7.9 %collective-permute-done.80 = bf16[1,36,16,128]{3,2,1,0:T(8,128)(2,1)S(1)} collective-permute-done((bf16[1,36,16,128]{3,2,1,0:T(8,128)(2,1)S(1)}, bf16[1,36,16,128]{3,2,1,0:T(8,128)(2,1)S(1)}, u32[]{:S(2)}, u32[]{:S(2)}) %collective-permute-start.80) | collective-permute-done | bytes 147488 | tf_op jit(solution)/shard_map/ppermute | solution.py:553
  271.9 8.0 %collective-permute-done.92 = bf16[1,36,16,128]{3,2,1,0:T(8,128)(2,1)S(1)} collective-permute-done((bf16[1,36,16,128]{3,2,1,0:T(8,128)(2,1)S(1)}, bf16[1,36,16,128]{3,2,1,0:T(8,128)(2,1)S(1)}, u32[]{:S(2)}, u32[]{:S(2)}) %collective-permute-start.92) | collective-permute-done | bytes 147488 | tf_op jit(solution)/shard_map/ppermute | solution.py:553
  283.9 10.9 %collective-permute-done.32 = bf16[8,20,16,128]{3,2,1,0:T(8,128)(2,1)S(1)} collective-permute-done((bf16[8,20,16,128]{3,2,1,0:T(8,128)(2,1)S(1)}, bf16[8,20,16,128]{3,2,1,0:T(8,128)(2,1)S(1)}, u32[]{:S(2)}, u32[]{:S(2)}) %collective-permute-start.32) | collective-permute-done | bytes 655392 | tf_op jit(solution)/shard_map/ppermute | solution.py:553
  297.2 6.5 %collective-permute-done.81 = bf16[2,36,16,128]{3,2,1,0:T(8,128)(2,1)S(1)} collective-permute-done((bf16[2,36,16,128]{3,2,1,0:T(8,128)(2,1)S(1)}, bf16[2,36,16,128]{3,2,1,0:T(8,128)(2,1)S(1)}, u32[]{:S(2)}, u32[]{:S(2)}) %collective-permute-start.81) | collective-permute-done | bytes 294944 | tf_op jit(solution)/shard_map/ppermute | solution.py:553
  316.4 5.0 %collective-permute-done.38 = bf16[2,18,16,128]{3,2,1,0:T(8,128)(2,1)S(1)} collective-permute-done((bf16[2,18,16,128]{3,2,1,0:T(8,128)(2,1)S(1)}, bf16[2,18,16,128]{3,2,1,0:T(8,128)(2,1)S(1)}, u32[]{:S(2)}, u32[]{:S(2)}) %collective-permute-start.38) | collective-permute-done | bytes 147488 | tf_op jit(solution)/shard_map/ppermute | solution.py:553
  323.9 8.4 %collective-permute-done.39 = bf16[1,18,16,128]{3,2,1,0:T(8,128)(2,1)S(1)} collective-permute-done((bf16[1,18,16,128]{3,2,1,0:T(8,128)(2,1)S(1)}, bf16[1,18,16,128]{3,2,1,0:T(8,128)(2,1)S(1)}, u32[]{:S(2)}, u32[]{:S(2)}) %collective-permute-start.39) | collective-permute-done | bytes 73760 | tf_op jit(solution)/shard_map/ppermute | solution.py:553
  333.1 4.6 collective-permute-done.26
  338.2 4.8 %collective-permute-done.30 = bf16[2,20,16,128]{3,2,1,0:T(8,128)(2,1)S(1)} collective-permute-done((bf16[2,20,16,128]{3,2,1,0:T(8,128)(2,1)S(1)}, bf16[2,20,16,128]{3,2,1,0:T(8,128)(2,1)S(1)}, u32[]{:S(2)}, u32[]{:S(2)}) %collective-permute-start.30) | collective-permute-done | bytes 163872 | tf_op jit(solution)/shard_map/ppermute | solution.py:553
  343.0 5.3 %collective-permute-done.34 = bf16[2,20,16,128]{3,2,1,0:T(8,128)(2,1)S(1)} collective-permute-done((bf16[2,20,16,128]{3,2,1,0:T(8,128)(2,1)S(1)}, bf16[2,20,16,128]{3,2,1,0:T(8,128)(2,1)S(1)}, u32[]{:S(2)}, u32[]{:S(2)}) %collective-permute-start.34) | collective-permute-done | bytes 163872 | tf_op jit(solution)/shard_map/ppermute | solution.py:553
  348.8 3.9 collective-permute-done.27
  359.6 4.3 collective-permute-done.35
  370.2 4.8 %collective-permute-done.82 = bf16[4,36,16,128]{3,2,1,0:T(8,128)(2,1)S(1)} collective-permute-done((bf16[4,36,16,128]{3,2,1,0:T(8,128)(2,1)S(1)}, bf16[4,36,16,128]{3,2,1,0:T(8,128)(2,1)S(1)}, u32[]{:S(2)}, u32[]{:S(2)}) %collective-permute-start.82) | collective-permute-done | bytes 589856 | tf_op jit(solution)/shard_map/ppermute | solution.py:553
  378.4 3.8 collective-permute-done.41
  385.8 16.5 %collective-permute-done.56 = bf16[1,18,16,128]{3,2,1,0:T(8,128)(2,1)S(1)} collective-permute-done((bf16[1,18,16,128]{3,2,1,0:T(8,128)(2,1)S(1)}, bf16[1,18,16,128]{3,2,1,0:T(8,128)(2,1)S(1)}, u32[]{:S(2)}, u32[]{:S(2)}) %collective-permute-start.56) | collective-permute-done | bytes 73760 | tf_op jit(solution)/shard_map/ppermute | solution.py:553
  406.6 4.0 collective-permute-done.57
  420.8 5.0 %collective-permute-done.45 = bf16[2,20,16,128]{3,2,1,0:T(8,128)(2,1)S(1)} collective-permute-done((bf16[2,20,16,128]{3,2,1,0:T(8,128)(2,1)S(1)}, bf16[2,20,16,128]{3,2,1,0:T(8,128)(2,1)S(1)}, u32[]{:S(2)}, u32[]{:S(2)}) %collective-permute-start.45) | collective-permute-done | bytes 163872 | tf_op jit(solution)/shard_map/ppermute | solution.py:553
  427.4 5.4 %collective-permute-done.50 = bf16[4,20,16,128]{3,2,1,0:T(8,128)(2,1)S(1)} collective-permute-done((bf16[4,20,16,128]{3,2,1,0:T(8,128)(2,1)S(1)}, bf16[4,20,16,128]{3,2,1,0:T(8,128)(2,1)S(1)}, u32[]{:S(2)}, u32[]{:S(2)}) %collective-permute-start.50) | collective-permute-done | bytes 327712 | tf_op jit(solution)/shard_map/ppermute | solution.py:553
  434.9 7.9 %collective-permute-done.54 = bf16[4,20,16,128]{3,2,1,0:T(8,128)(2,1)S(1)} collective-permute-done((bf16[4,20,16,128]{3,2,1,0:T(8,128)(2,1)S(1)}, bf16[4,20,16,128]{3,2,1,0:T(8,128)(2,1)S(1)}, u32[]{:S(2)}, u32[]{:S(2)}) %collective-permute-start.54) | collective-permute-done | bytes 327712 | tf_op jit(solution)/shard_map/ppermute | solution.py:553
  444.1 7.7 %collective-permute-done.46 = bf16[4,20,16,128]{3,2,1,0:T(8,128)(2,1)S(1)} collective-permute-done((bf16[4,20,16,128]{3,2,1,0:T(8,128)(2,1)S(1)}, bf16[4,20,16,128]{3,2,1,0:T(8,128)(2,1)S(1)}, u32[]{:S(2)}, u32[]{:S(2)}) %collective-permute-start.46) | collective-permute-done | bytes 327712 | tf_op jit(solution)/shard_map/ppermute | solution.py:553
  454.4 4.7 collective-permute-start.55
  461.1 10.7 %shard_map.243 = (f32[384,4096]{1,0:T(8,128)}, f32[384,4096]{1,0:T(8,128)}, f32[1024,1536]{1,0:T(8,128)}) custom-call(s32[3]{0:T(128)S(1)} %pad_add_fusion.at_ref, bf16[8,36,16,128]{3,2,1,0:T(8,128)(2,1)S(1)} %pad_maximum_fusion.9.refs_0_, bf16[8,36,16,128]{3,2,1,0:T(8,128)(2,1)S(1)} %collective-permute-done.83.refs_1_, ...), custom_call_target="tpu_custom_call" | custom-call | bytes 29360128 | tf_op jit(solution)/shard_map/pallas_call | solution.py:416
  471.9 4.7 shard_map.241
  (437 shorter events, 218.8 us)
Async XLA Ops:
  0.7 32.5 %collective-permute-start.10 = (bf16[128,1536]{1,0:T(8,128)(2,1)}, bf16[128,1536]{1,0:T(8,128)(2,1)S(1)}, u32[]{:S(2)}, u32[]{:S(2)}) collective-permute-start(bf16[128,1536]{1,0:T(8,128)(2,1)} %param.27), channel_id=1, source_target_pairs={{0,2},{1,3},{4,6},{5,7},{8,10},{9,11},{12,14},{13,15},{2,0},{3,1},... | collective-permute-start | bytes 1179656 | tf_op jit(solution)/shard_map/ppermute | solution.py:553
  4.5 30.3 %collective-permute-start = (bf16[144,1536]{1,0:T(8,128)(2,1)}, bf16[144,1536]{1,0:T(8,128)(2,1)S(1)}, u32[]{:S(2)}, u32[]{:S(2)}) collective-permute-start(bf16[144,1536]{1,0:T(8,128)(2,1)} %get-tuple-element.135), channel_id=1, source_target_pairs={{0,2},{1,3},{4,6},{5,7},{8,10},{9,11},{12,14},{13,15},{2,0},{3,1},... | collective-permute-start | bytes 1327112 | tf_op jit(solution)/shard_map/ppermute | solution.py:553
  13.7 24.6 %collective-permute-start.3 = (bf16[144,2560]{1,0:T(8,128)(2,1)}, bf16[144,2560]{1,0:T(8,128)(2,1)}, u32[]{:S(2)}, u32[]{:S(2)}) collective-permute-start(bf16[144,2560]{1,0:T(8,128)(2,1)} %slice.1075), channel_id=1, source_target_pairs={{0,2},{1,3},{4,6},{5,7},{8,10},{9,11},{12,14},{13,15},{2,0},{3,1},... | collective-permute-start | bytes 2211848 | tf_op jit(solution)/shard_map/ppermute | solution.py:553
  17.4 29.2 %collective-permute-start.4 = (bf16[240,2560]{1,0:T(8,128)(2,1)}, bf16[240,2560]{1,0:T(8,128)(2,1)S(1)}, u32[]{:S(2)}, u32[]{:S(2)}) collective-permute-start(bf16[240,2560]{1,0:T(8,128)(2,1)} %slice.1077), channel_id=1, source_target_pairs={{0,18},{1,19},{4,22},{5,23},{8,26},{9,27},{12,30},{13,31},{2,16},{... | collective-permute-start | bytes 3686408 | tf_op jit(solution)/shard_map/ppermute | solution.py:553
  33.2 39.7 %collective-permute-start.13 = (bf16[128,4096]{1,0:T(8,128)(2,1)}, bf16[128,4096]{1,0:T(8,128)(2,1)}, u32[]{:S(2)}, u32[]{:S(2)}) collective-permute-start(bf16[128,4096]{1,0:T(8,128)(2,1)} %pad_maximum_fusion.13), channel_id=1, source_target_pairs={{0,2},{1,3},{4,6},{5,7},{8,10},{9,11},{12,14},{13,15},{2,0},{3,1},... | collective-permute-start | bytes 3145736 | tf_op jit(solution)/shard_map/ppermute | solution.py:553
  34.8 31.2 %collective-permute-start.12 = (bf16[384,2048]{1,0:T(8,128)(2,1)}, bf16[384,2048]{1,0:T(8,128)(2,1)}, u32[]{:S(2)}, u32[]{:S(2)}) collective-permute-start(bf16[384,2048]{1,0:T(8,128)(2,1)} %pad_maximum_fusion.7), channel_id=1, source_target_pairs={{0,1},{1,0},{4,5},{5,4},{8,9},{9,8},{12,13},{13,12},{2,3},{3,2},{6... | collective-permute-start | bytes 4718600 | tf_op jit(solution)/shard_map/ppermute | solution.py:553
  36.0 27.9 %collective-permute-start.11 = (bf16[2,128,1536]{2,1,0:T(8,128)(2,1)S(1)}, bf16[2,128,1536]{2,1,0:T(8,128)(2,1)S(1)}, u32[]{:S(2)}, u32[]{:S(2)}) collective-permute-start(bf16[2,128,1536]{2,1,0:T(8,128)(2,1)S(1)} %pad_maximum_fusion.15), channel_id=1, source_target_pairs={{0,1},{1,0},{4,5},{5,4},{8,9},{9,8},{12,13},{13,12},{2,3},{3,2},{6... | collective-permute-start | bytes 2359304 | tf_op jit(solution)/shard_map/ppermute | solution.py:553
  48.3 48.0 %collective-permute-start.14 = (bf16[256,4096]{1,0:T(8,128)(2,1)}, bf16[256,4096]{1,0:T(8,128)(2,1)}, u32[]{:S(2)}, u32[]{:S(2)}) collective-permute-start(bf16[256,4096]{1,0:T(8,128)(2,1)} %pad_maximum_fusion), channel_id=1, source_target_pairs={{0,18},{1,19},{4,22},{5,23},{8,26},{9,27},{12,30},{13,31},{2,16},{... | collective-permute-start | bytes 6291464 | tf_op jit(solution)/shard_map/ppermute | solution.py:553
  70.1 29.1 %collective-permute-start.8 = (bf16[256,1536]{1,0:T(8,128)(2,1)S(1)}, bf16[256,1536]{1,0:T(8,128)(2,1)S(1)}, u32[]{:S(2)}, u32[]{:S(2)}) collective-permute-start(bf16[256,1536]{1,0:T(8,128)(2,1)S(1)} %add_convert_fusion.3), channel_id=1, source_target_pairs={{0,2},{1,3},{4,6},{5,7},{8,10},{9,11},{12,14},{13,15},{2,0},{3,1},... | collective-permute-start | bytes 2359304 | tf_op jit(solution)/shard_map/ppermute | solution.py:553
  74.9 28.5 %collective-permute-start.15 = (bf16[128,2048]{1,0:T(8,128)(2,1)S(1)}, bf16[128,2048]{1,0:T(8,128)(2,1)S(1)}, u32[]{:S(2)}, u32[]{:S(2)}) collective-permute-start(bf16[128,2048]{1,0:T(8,128)(2,1)S(1)} %get-tuple-element.124), channel_id=1, source_target_pairs={{0,1},{1,0},{4,5},{5,4},{8,9},{9,8},{12,13},{13,12},{2,3},{3,2},{6... | collective-permute-start | bytes 1572872 | tf_op jit(solution)/shard_map/ppermute | solution.py:553
  126.6 20.6 %collective-permute-start.19 = (bf16[256,1536]{1,0:T(8,128)(2,1)S(1)}, bf16[256,1536]{1,0:T(8,128)(2,1)S(1)}, u32[]{:S(2)}, u32[]{:S(2)}) collective-permute-start(bf16[256,1536]{1,0:T(8,128)(2,1)S(1)} %get-tuple-element.57), channel_id=1, source_target_pairs={{0,1},{1,0},{4,5},{5,4},{8,9},{9,8},{12,13},{13,12},{2,3},{3,2},{6... | collective-permute-start | bytes 2359304 | tf_op jit(solution)/shard_map/ppermute | solution.py:553
  130.5 21.4 %collective-permute-start.17 = (bf16[256,1536]{1,0:T(8,128)(2,1)S(1)}, bf16[256,1536]{1,0:T(8,128)(2,1)}, u32[]{:S(2)}, u32[]{:S(2)}) collective-permute-start(bf16[256,1536]{1,0:T(8,128)(2,1)S(1)} %slice.1089), channel_id=1, source_target_pairs={{0,1},{1,0},{4,5},{5,4},{8,9},{9,8},{12,13},{13,12},{2,3},{3,2},{6... | collective-permute-start | bytes 2359304 | tf_op jit(solution)/shard_map/ppermute | solution.py:553
  141.8 29.0 %collective-permute-start.60 = (bf16[8,36,16,128]{3,2,1,0:T(8,128)(2,1)S(1)}, bf16[8,36,16,128]{3,2,1,0:T(8,128)(2,1)S(1)}, u32[]{:S(2)}, u32[]{:S(2)}) collective-permute-start(bf16[8,36,16,128]{3,2,1,0:T(8,128)(2,1)S(1)} %get-tuple-element.83), channel_id=1, source_target_pairs={{0,4},{1,5},{4,0},{5,1},{8,12},{9,13},{12,8},{13,9},{2,6},{3,7},{6... | collective-permute-start | bytes 3538952 | tf_op jit(solution)/shard_map/ppermute | solution.py:553
  144.3 30.2 %collective-permute-start.64 = (bf16[8,36,16,128]{3,2,1,0:T(8,128)(2,1)}, bf16[8,36,16,128]{3,2,1,0:T(8,128)(2,1)S(1)}, u32[]{:S(2)}, u32[]{:S(2)}) collective-permute-start(bf16[8,36,16,128]{3,2,1,0:T(8,128)(2,1)} %get-tuple-element.85), channel_id=1, source_target_pairs={{0,12},{1,13},{4,8},{5,9},{8,4},{9,5},{12,0},{13,1},{2,14},{3,15},... | collective-permute-start | bytes 3538952 | tf_op jit(solution)/shard_map/ppermute | solution.py:553
  146.8 31.9 %collective-permute-start.68 = (bf16[8,36,16,128]{3,2,1,0:T(8,128)(2,1)}, bf16[8,36,16,128]{3,2,1,0:T(8,128)(2,1)S(1)}, u32[]{:S(2)}, u32[]{:S(2)}) collective-permute-start(bf16[8,36,16,128]{3,2,1,0:T(8,128)(2,1)} %get-tuple-element.87), channel_id=1, source_target_pairs={{0,32},{1,33},{4,36},{5,37},{8,40},{9,41},{12,44},{13,45},{2,34},{... | collective-permute-start | bytes 3538952 | tf_op jit(solution)/shard_map/ppermute | solution.py:553
  148.1 30.8 %collective-permute-start.72 = (bf16[8,36,16,128]{3,2,1,0:T(8,128)(2,1)}, bf16[8,36,16,128]{3,2,1,0:T(8,128)(2,1)S(1)}, u32[]{:S(2)}, u32[]{:S(2)}) collective-permute-start(bf16[8,36,16,128]{3,2,1,0:T(8,128)(2,1)} %get-tuple-element.89), channel_id=1, source_target_pairs={{0,96},{1,97},{4,100},{5,101},{8,104},{9,105},{12,108},{13,109},{2... | collective-permute-start | bytes 3538952 | tf_op jit(solution)/shard_map/ppermute | solution.py:553
  151.8 28.9 %collective-permute-start.20 = (bf16[256,1536]{1,0:T(8,128)(2,1)S(1)}, bf16[256,1536]{1,0:T(8,128)(2,1)S(1)}, u32[]{:S(2)}, u32[]{:S(2)}) collective-permute-start(bf16[256,1536]{1,0:T(8,128)(2,1)S(1)} %add_convert_fusion.1), channel_id=1, source_target_pairs={{0,2},{1,3},{4,6},{5,7},{8,10},{9,11},{12,14},{13,15},{2,0},{3,1},... | collective-permute-start | bytes 2359304 | tf_op jit(solution)/shard_map/ppermute | solution.py:553
  170.8 88.7 %collective-permute-start.18 = (bf16[128,1536]{1,0:T(8,128)(2,1)}, bf16[128,1536]{1,0:T(8,128)(2,1)}, u32[]{:S(2)}, u32[]{:S(2)}) collective-permute-start(bf16[128,1536]{1,0:T(8,128)(2,1)} %slice.1091), channel_id=1, source_target_pairs={{0,2},{1,3},{4,6},{5,7},{8,10},{9,11},{12,14},{13,15},{2,0},{3,1},... | collective-permute-start | bytes 1179656 | tf_op jit(solution)/shard_map/ppermute | solution.py:553
  191.3 30.4 %collective-permute-start.21 = (bf16[256,1536]{1,0:T(8,128)(2,1)S(1)}, bf16[256,1536]{1,0:T(8,128)(2,1)S(1)}, u32[]{:S(2)}, u32[]{:S(2)}) collective-permute-start(bf16[256,1536]{1,0:T(8,128)(2,1)S(1)} %get-tuple-element.99), channel_id=1, source_target_pairs={{0,1},{1,0},{4,5},{5,4},{8,9},{9,8},{12,13},{13,12},{2,3},{3,2},{6... | collective-permute-start | bytes 2359304 | tf_op jit(solution)/shard_map/ppermute | solution.py:553
  252.4 29.0 %collective-permute-start.36 = (bf16[8,18,16,128]{3,2,1,0:T(8,128)(2,1)S(1)}, bf16[8,18,16,128]{3,2,1,0:T(8,128)(2,1)S(1)}, u32[]{:S(2)}, u32[]{:S(2)}) collective-permute-start(bf16[8,18,16,128]{3,2,1,0:T(8,128)(2,1)S(1)} %get-tuple-element.74), channel_id=1, source_target_pairs={{0,96},{1,97},{4,100},{5,101},{8,104},{9,105},{12,108},{13,109},{2... | collective-permute-start | bytes 1769480 | tf_op jit(solution)/shard_map/ppermute | solution.py:553
  261.4 21.9 %collective-permute-start.28 = (bf16[8,20,16,128]{3,2,1,0:T(8,128)(2,1)S(1)}, bf16[8,20,16,128]{3,2,1,0:T(8,128)(2,1)S(1)}, u32[]{:S(2)}, u32[]{:S(2)}) collective-permute-start(bf16[8,20,16,128]{3,2,1,0:T(8,128)(2,1)S(1)} %get-tuple-element.70), channel_id=1, source_target_pairs={{0,12},{1,13},{4,8},{5,9},{8,4},{9,5},{12,0},{13,1},{2,14},{3,15},... | collective-permute-start | bytes 1966088 | tf_op jit(solution)/shard_map/ppermute | solution.py:553
  281.4 24.5 %collective-permute-start.89 = (bf16[2,36,16,128]{3,2,1,0:T(8,128)(2,1)S(1)}, bf16[2,36,16,128]{3,2,1,0:T(8,128)(2,1)S(1)}, u32[]{:S(2)}, u32[]{:S(2)}) collective-permute-start(bf16[2,36,16,128]{3,2,1,0:T(8,128)(2,1)S(1)} %pad_maximum_fusion.31), channel_id=1, source_target_pairs={{0,4},{1,5},{4,0},{5,1},{8,12},{9,13},{12,8},{13,9},{2,6},{3,7},{6... | collective-permute-start | bytes 884744 | tf_op jit(solution)/shard_map/ppermute | solution.py:553
  281.9 23.4 %collective-permute-start.93 = (bf16[2,36,16,128]{3,2,1,0:T(8,128)(2,1)S(1)}, bf16[2,36,16,128]{3,2,1,0:T(8,128)(2,1)S(1)}, u32[]{:S(2)}, u32[]{:S(2)}) collective-permute-start(bf16[2,36,16,128]{3,2,1,0:T(8,128)(2,1)S(1)} %pad_maximum_fusion.32), channel_id=1, source_target_pairs={{0,12},{1,13},{4,8},{5,9},{8,4},{9,5},{12,0},{13,1},{2,14},{3,15},... | collective-permute-start | bytes 884744 | tf_op jit(solution)/shard_map/ppermute | solution.py:553
  283.3 21.8 %collective-permute-start.85 = (bf16[2,36,16,128]{3,2,1,0:T(8,128)(2,1)S(1)}, bf16[2,36,16,128]{3,2,1,0:T(8,128)(2,1)S(1)}, u32[]{:S(2)}, u32[]{:S(2)}) collective-permute-start(bf16[2,36,16,128]{3,2,1,0:T(8,128)(2,1)S(1)} %pad_maximum_fusion.30), channel_id=1, source_target_pairs={{0,96},{1,97},{4,100},{5,101},{8,104},{9,105},{12,108},{13,109},{2... | collective-permute-start | bytes 884744 | tf_op jit(solution)/shard_map/ppermute | solution.py:553
  306.0 59.4 %collective-permute-start.23 = (bf16[128,1536]{1,0:T(8,128)(2,1)S(1)}, bf16[128,1536]{1,0:T(8,128)(2,1)S(1)}, u32[]{:S(2)}, u32[]{:S(2)}) collective-permute-start(bf16[128,1536]{1,0:T(8,128)(2,1)S(1)} %slice.1097), channel_id=1, source_target_pairs={{0,2},{1,3},{4,6},{5,7},{8,10},{9,11},{12,14},{13,15},{2,0},{3,1},... | collective-permute-start | bytes 1179656 | tf_op jit(solution)/shard_map/ppermute | solution.py:553
  309.3 104.5 %collective-permute-start.90 = (bf16[4,36,16,128]{3,2,1,0:T(8,128)(2,1)S(1)}, bf16[4,36,16,128]{3,2,1,0:T(8,128)(2,1)S(1)}, u32[]{:S(2)}, u32[]{:S(2)}) collective-permute-start(bf16[4,36,16,128]{3,2,1,0:T(8,128)(2,1)S(1)} %pad_maximum_fusion.23), channel_id=1, source_target_pairs={{0,96},{1,97},{4,100},{5,101},{8,104},{9,105},{12,108},{13,109},{2... | collective-permute-start | bytes 1769480 | tf_op jit(solution)/shard_map/ppermute | solution.py:553
  313.6 56.3 %collective-permute-start.94 = (bf16[4,36,16,128]{3,2,1,0:T(8,128)(2,1)S(1)}, bf16[4,36,16,128]{3,2,1,0:T(8,128)(2,1)S(1)}, u32[]{:S(2)}, u32[]{:S(2)}) collective-permute-start(bf16[4,36,16,128]{3,2,1,0:T(8,128)(2,1)S(1)} %pad_maximum_fusion.24), channel_id=1, source_target_pairs={{0,32},{1,33},{4,36},{5,37},{8,40},{9,41},{12,44},{13,45},{2,34},{... | collective-permute-start | bytes 1769480 | tf_op jit(solution)/shard_map/ppermute | solution.py:553
  321.5 56.6 %collective-permute-start.86 = (bf16[4,36,16,128]{3,2,1,0:T(8,128)(2,1)S(1)}, bf16[4,36,16,128]{3,2,1,0:T(8,128)(2,1)S(1)}, u32[]{:S(2)}, u32[]{:S(2)}) collective-permute-start(bf16[4,36,16,128]{3,2,1,0:T(8,128)(2,1)S(1)} %pad_maximum_fusion.22), channel_id=1, source_target_pairs={{0,4},{1,5},{4,0},{5,1},{8,12},{9,13},{12,8},{13,9},{2,6},{3,7},{6... | collective-permute-start | bytes 1769480 | tf_op jit(solution)/shard_map/ppermute | solution.py:553
  378.1 76.2 %collective-permute-start.83 = (bf16[8,36,16,128]{3,2,1,0:T(8,128)(2,1)S(1)}, bf16[8,36,16,128]{3,2,1,0:T(8,128)(2,1)S(1)}, u32[]{:S(2)}, u32[]{:S(2)}) collective-permute-start(bf16[8,36,16,128]{3,2,1,0:T(8,128)(2,1)S(1)} %pad_maximum_fusion.9.refs_0_), channel_id=1, source_target_pairs={{0,4},{1,5},{4,0},{5,1},{8,12},{9,13},{12,8},{13,9},{2,6},{3,7},{6... | collective-permute-start | bytes 3538952 | tf_op jit(solution)/shard_map/ppermute | solution.py:553
  413.8 40.6 %collective-permute-start.87 = (bf16[8,36,16,128]{3,2,1,0:T(8,128)(2,1)S(1)}, bf16[8,36,16,128]{3,2,1,0:T(8,128)(2,1)S(1)}, u32[]{:S(2)}, u32[]{:S(2)}) collective-permute-start(bf16[8,36,16,128]{3,2,1,0:T(8,128)(2,1)S(1)} %pad_maximum_fusion.10.refs_2_), channel_id=1, source_target_pairs={{0,12},{1,13},{4,8},{5,9},{8,4},{9,5},{12,0},{13,1},{2,14},{3,15},... | collective-permute-start | bytes 3538952 | tf_op jit(solution)/shard_map/ppermute | solution.py:553
  415.8 43.3 %collective-permute-start.95 = (bf16[8,36,16,128]{3,2,1,0:T(8,128)(2,1)S(1)}, bf16[8,36,16,128]{3,2,1,0:T(8,128)(2,1)S(1)}, u32[]{:S(2)}, u32[]{:S(2)}) collective-permute-start(bf16[8,36,16,128]{3,2,1,0:T(8,128)(2,1)S(1)} %pad_maximum_fusion.12.refs_6_), channel_id=1, source_target_pairs={{0,96},{1,97},{4,100},{5,101},{8,104},{9,105},{12,108},{13,109},{2... | collective-permute-start | bytes 3538952 | tf_op jit(solution)/shard_map/ppermute | solution.py:553
  432.8 28.3 %collective-permute-start.91 = (bf16[8,36,16,128]{3,2,1,0:T(8,128)(2,1)S(1)}, bf16[8,36,16,128]{3,2,1,0:T(8,128)(2,1)}, u32[]{:S(2)}, u32[]{:S(2)}) collective-permute-start(bf16[8,36,16,128]{3,2,1,0:T(8,128)(2,1)S(1)} %pad_maximum_fusion.11.refs_4_), channel_id=1, source_target_pairs={{0,32},{1,33},{4,36},{5,37},{8,40},{9,41},{12,44},{13,45},{2,34},{... | collective-permute-start | bytes 3538952 | tf_op jit(solution)/shard_map/ppermute | solution.py:553
  (101 other events, 1013.2 us)
